TPU v7x, 32 devices: a whole 2x2x4 slice. The times are simulated.
32 devices in a mesh: rows: 8 (over y, x, core), batch: 4 (over z).
Axes of the slice: x: 2, y: 2, z: 4, core: 2. Of those that a mesh axis runs over, the one named last changes fastest.
Arguments:
- layer_input: bfloat16 [8, 128, 128, 256], P('batch', 'rows'), may hold values from -6 to 6
- hidden_state: bfloat16 [8, 128, 128, 256], P('batch', 'rows'), may hold values from -6 to 6
- crop_rows: int32 [8], P('batch'), may hold values from 113 to 128, as said below
- crop_cols: int32 [8], P('batch'), may hold values from 64 to 128, as said below
- first_gain: float32 [256], replicated, may hold values from 0.1 to 1.9
- first_shift: float32 [256], replicated, may hold values from -3 to 3
- qkv_weight: float32 [256, 768], P(('rows', 'batch')), may hold values from -0.375 to 0.375
- bias_table: float32 [225, 8], replicated, may hold values from -4 to 4
- output_weight: float32 [256, 256], P(('rows', 'batch')), may hold values from -1 to 1
- output_bias: float32 [256], replicated, may hold values from -3 to 3
- second_gain: float32 [256], replicated, may hold values from 0.1 to 1.9
- second_shift: float32 [256], replicated, may hold values from -3 to 3
- up_weight: float32 [256, 1024], P(('rows', 'batch')), may hold values from -0.375 to 0.375
- up_bias: float32 [1024], replicated, may hold values from -3 to 3
- down_weight: float32 [1024, 256], P(('rows', 'batch')), may hold values from -0.1875 to 0.1875
- down_bias: float32 [256], replicated, may hold values from -3 to 3
- conv_weight: float32 [4608, 256], P(('rows', 'batch')), may hold values from -0.09375 to 0.09375
- conv_bias: float32 [256], replicated, may hold values from -3 to 3
- cotangent: bfloat16 [8, 128, 128, 256], P('batch', 'rows'), may hold values from -6 to 6
Outputs:
- layer_output: bfloat16 [8, 128, 128, 256], P('batch', 'rows')
- input_grad: float32 [8, 128, 128, 256], P('batch', 'rows')
- hidden_grad: float32 [8, 128, 128, 256], P('batch', 'rows')
- first_gain_grad: float32 [256], replicated
- first_shift_grad: float32 [256], replicated
- qkv_weight_grad: float32 [256, 768], P(('rows', 'batch'))
- bias_table_grad: float32 [225, 8], replicated
- output_weight_grad: float32 [256, 256], P(('rows', 'batch'))
- output_bias_grad: float32 [256], replicated
- second_gain_grad: float32 [256], replicated
- second_shift_grad: float32 [256], replicated
- up_weight_grad: float32 [256, 1024], P(('rows', 'batch'))
- up_bias_grad: float32 [1024], replicated
- down_weight_grad: float32 [1024, 256], P(('rows', 'batch'))
- down_bias_grad: float32 [256], replicated
- conv_weight_grad: float32 [4608, 256], P(('rows', 'batch'))
- conv_bias_grad: float32 [256], replicated
Inputs may be any that keep to these rules, and one draw needn't show every extreme that they name: `crop_rows`: every crop reaches into the last 16 rows of the grid; one crop of the batch has all 128 rows. `crop_cols`: some crop has all 128 columns.
All inputs are finite; a program needn't handle non-finite values.
Results may differ from a plain program's by a relative error of at most 0.012.
The roundings to bfloat16 on the way count: a program that leaves them out, or rounds other values in their place, can miss the bound.
Values may be sent and summed in bfloat16 or wider, within the bound.
No kernel may reach another device: no remote copies, remote signals or barrier semaphores. Data moves between devices by JAX's collectives and lax.ppermute only.
A program may use at most 320 MiB of HBM per device.

v0:
```python
import jax
import jax.numpy as jnp
from jax import lax
from jax.sharding import PartitionSpec as P

WIN = 8


HIGHEST = lax.Precision.HIGHEST
EPSILON = 1e-05
MASKED = -100.0


def from_behind(x, axis, by):
    devices = lax.axis_size(axis)
    return lax.ppermute(x, axis, [(i, (i + by) % devices) for i in range(devices)])


def padded_2(x, sides, width):
    for axis, dim in sides:
        devices, length = (lax.axis_size(axis), x.shape[dim])
        up = [(i, (i + 1) % devices) for i in range(devices - 1)]
        down = [(j, i) for i, j in up]
        last = lax.slice_in_dim(x, length - width, length, axis=dim)
        initial = lax.slice_in_dim(x, 0, width, axis=dim)
        before = lax.ppermute(last, axis, up)
        after = lax.ppermute(initial, axis, down)
        x = jnp.concatenate([before, x, after], axis=dim)
    return x


def layer_norm(features, gain_vec, offset_vec):
    centred = features - jnp.mean(features, -1, keepdims=True)
    spread = jnp.mean(centred * centred, -1, keepdims=True)
    return centred * lax.rsqrt(spread + EPSILON) * gain_vec + offset_vec


def gelu_exact(features):
    return jax.nn.gelu(features, approximate=False)


def to_windows(field):
    samples, grid_rows, grid_cols, channels = field.shape
    blocks = field.reshape(samples, grid_rows // WIN, WIN, grid_cols // WIN, WIN, channels)
    return blocks.transpose(0, 1, 3, 2, 4, 5).reshape(-1, WIN * WIN, channels)


def from_windows(windowed, samples, grid_rows, grid_cols):
    channels = windowed.shape[-1]
    blocks = windowed.reshape(samples, grid_rows // WIN, grid_cols // WIN, WIN, WIN, channels)
    return blocks.transpose(0, 1, 3, 2, 4, 5).reshape(samples, grid_rows, grid_cols, channels)


def position_onehot():
    places = jnp.arange(WIN * WIN)
    place_row = places // WIN
    place_col = places % WIN
    offsets = (place_row[:, None] - place_row[None, :] + WIN - 1) * (2 * WIN - 1) + (
        place_col[:, None] - place_col[None, :] + WIN - 1
    )
    return (offsets.reshape(-1)[:, None] == jnp.arange((2 * WIN - 1) ** 2)[None, :]).astype(
        jnp.float32
    )


def window_scores(queries, key_part, pos_bias, score_mask, score_scale):
    scores = jnp.einsum("wqhe,wkhe->whqk", queries, key_part, preferred_element_type=jnp.float32)
    return scores * score_scale + pos_bias[None] + score_mask[:, None]


def shards(
    layer_input,
    hidden_state,
    crop_rows,
    crop_cols,
    first_gain,
    first_shift,
    qkv_weight,
    bias_table,
    output_weight,
    output_bias,
    second_gain,
    second_shift,
    up_weight,
    up_bias,
    down_weight,
    down_bias,
    conv_weight,
    conv_bias,
    cotangent,
):
    samples, grid_rows, grid_cols, model_width = layer_input.shape
    head_count = bias_table.shape[1]
    head_size = model_width // head_count
    score_scale = head_size ** (-0.5)
    half_win = WIN // 2
    joined_width = 2 * model_width
    height = grid_rows * lax.axis_size("rows")
    row_start = lax.axis_index("rows") * grid_rows
    col_ids = jnp.arange(grid_cols)
    own_rows = row_start + jnp.arange(grid_rows)
    validity = (
        (own_rows[None, :, None] < crop_rows[:, None, None])
        & (col_ids[None, None, :] < crop_cols[:, None, None])
    ).astype(jnp.float32)
    frame_rows = (row_start - half_win + jnp.arange(grid_rows)) % height
    frame_cols = (col_ids - half_win) % grid_cols
    frame_valid = (
        (frame_rows[None, :, None] < crop_rows[:, None, None])
        & (frame_cols[None, None, :] < crop_cols[:, None, None])
    ).astype(jnp.float32)
    region = 2 * (frame_rows[:, None] >= height - half_win).astype(jnp.int32) + (
        frame_cols[None, :] >= grid_cols - half_win
    ).astype(jnp.int32)
    region = jnp.broadcast_to(region[None, :, :, None], (samples, grid_rows, grid_cols, 1))
    region_win = to_windows(region)[..., 0]
    valid_win = to_windows(frame_valid[..., None])[..., 0]
    score_mask = MASKED * (region_win[:, :, None] != region_win[:, None, :]).astype(
        jnp.float32
    ) + MASKED * (1.0 - valid_win[:, None, :])
    onehot = position_onehot()
    pos_bias = (
        jnp.dot(onehot, bias_table, precision=HIGHEST)
        .reshape(WIN * WIN, WIN * WIN, head_count)
        .transpose(2, 0, 1)
    )
    qkv_full, output_full, up_full, down_full, conv_full = (
        lax.all_gather(qkv_weight.astype(jnp.bfloat16), ("rows", "batch"), axis=0, tiled=True),
        lax.all_gather(output_weight.astype(jnp.bfloat16), ("rows", "batch"), axis=0, tiled=True),
        lax.all_gather(up_weight.astype(jnp.bfloat16), ("rows", "batch"), axis=0, tiled=True),
        lax.all_gather(down_weight.astype(jnp.bfloat16), ("rows", "batch"), axis=0, tiled=True),
        lax.all_gather(conv_weight.astype(jnp.bfloat16), ("rows", "batch"), axis=0, tiled=True),
    )
    inputs = layer_input.astype(jnp.float32)
    normed = layer_norm(inputs, first_gain, first_shift).astype(jnp.bfloat16)
    from_above = from_behind(normed[:, grid_rows - half_win :], "rows", 1)
    framed = jnp.roll(
        jnp.concatenate([from_above, normed[:, : grid_rows - half_win]], 1), half_win, 2
    )
    windowed = to_windows(framed)
    window_count = windowed.shape[0]
    projected = jnp.einsum(
        "wtd,df->wtf", windowed, qkv_full, preferred_element_type=jnp.float32
    ).astype(jnp.bfloat16)
    queries = projected[..., :model_width].reshape(window_count, WIN * WIN, head_count, head_size)
    key_part = projected[..., model_width : 2 * model_width].reshape(
        window_count, WIN * WIN, head_count, head_size
    )
    value_part = projected[..., 2 * model_width :].reshape(
        window_count, WIN * WIN, head_count, head_size
    )
    scores = window_scores(queries, key_part, pos_bias, score_mask, score_scale)
    top_score = jnp.max(scores, -1, keepdims=True)
    log_total = top_score + jnp.log(jnp.sum(jnp.exp(scores - top_score), -1, keepdims=True))
    probs_low = jnp.exp(scores - log_total).astype(jnp.bfloat16)
    combined = jnp.einsum(
        "whqk,wkhe->wqhe", probs_low, value_part, preferred_element_type=jnp.float32
    ).astype(jnp.bfloat16)
    combined = jnp.roll(
        from_windows(
            combined.reshape(window_count, WIN * WIN, model_width), samples, grid_rows, grid_cols
        ),
        -half_win,
        2,
    )
    from_below = from_behind(combined[:, :half_win], "rows", -1)
    combined_own = jnp.concatenate([combined[:, half_win:], from_below], 1)
    first_sum = (
        inputs
        + jnp.einsum("srcd,de->srce", combined_own, output_full, preferred_element_type=jnp.float32)
        + output_bias
    )
    second_norm = layer_norm(first_sum, second_gain, second_shift).astype(jnp.bfloat16)
    raised = (
        jnp.einsum("srcd,df->srcf", second_norm, up_full, preferred_element_type=jnp.float32)
        + up_bias
    )
    activated = gelu_exact(raised).astype(jnp.bfloat16)
    second_sum = (
        first_sum
        + jnp.einsum("srcf,fd->srcd", activated, down_full, preferred_element_type=jnp.float32)
        + down_bias
    )
    joined = (
        jnp.concatenate([second_sum, hidden_state.astype(jnp.float32)], -1) * validity[..., None]
    ).astype(jnp.bfloat16)
    rimmed = padded_2(joined, (("rows", 1),), 1)
    padded = jnp.pad(rimmed, ((0, 0), (0, 0), (1, 1), (0, 0)))
    summed = conv_bias
    for tap_row in range(3):
        for tap_col in range(3):
            first_row = (tap_row * 3 + tap_col) * joined_width
            window_slice = padded[:, tap_row : tap_row + grid_rows, tap_col : tap_col + grid_cols]
            summed = summed + jnp.einsum(
                "srcx,xy->srcy",
                window_slice,
                conv_full[first_row : first_row + joined_width],
                preferred_element_type=jnp.float32,
            )
    layer_output = (summed * validity[..., None]).astype(jnp.bfloat16)
    qkv_full, output_full, up_full, down_full, conv_full = (
        lax.all_gather(qkv_weight.astype(jnp.bfloat16), ("rows", "batch"), axis=0, tiled=True),
        lax.all_gather(output_weight.astype(jnp.bfloat16), ("rows", "batch"), axis=0, tiled=True),
        lax.all_gather(up_weight.astype(jnp.bfloat16), ("rows", "batch"), axis=0, tiled=True),
        lax.all_gather(down_weight.astype(jnp.bfloat16), ("rows", "batch"), axis=0, tiled=True),
        lax.all_gather(conv_weight.astype(jnp.bfloat16), ("rows", "batch"), axis=0, tiled=True),
    )
    out_grad = (cotangent.astype(jnp.float32) * validity[..., None]).astype(jnp.bfloat16)
    grad_rimmed = padded_2(out_grad, (("rows", 1),), 1)
    grad_padded = jnp.pad(grad_rimmed, ((0, 0), (0, 0), (1, 1), (0, 0)))
    joined_grad = jnp.zeros(joined.shape, jnp.float32)
    conv_pieces = []
    for tap_row in range(3):
        for tap_col in range(3):
            first_row = (tap_row * 3 + tap_col) * joined_width
            grad_slice = grad_padded[
                :, 2 - tap_row : 2 - tap_row + grid_rows, 2 - tap_col : 2 - tap_col + grid_cols
            ]
            joined_grad = joined_grad + jnp.einsum(
                "srcy,xy->srcx",
                grad_slice,
                conv_full[first_row : first_row + joined_width],
                preferred_element_type=jnp.float32,
            )
            window_slice = padded[:, tap_row : tap_row + grid_rows, tap_col : tap_col + grid_cols]
            conv_pieces.append(
                jnp.einsum(
                    "srcx,srcy->xy", window_slice, out_grad, preferred_element_type=jnp.float32
                )
            )
    conv_local = jnp.concatenate(conv_pieces, 0)
    conv_bias_local = jnp.sum(out_grad.astype(jnp.float32), (0, 1, 2))
    joined_grad = joined_grad * validity[..., None]
    hidden_grad = joined_grad[..., model_width:]
    second_grad = joined_grad[..., :model_width]
    branch_grad = second_grad.astype(jnp.bfloat16)
    down_local = jnp.einsum(
        "srcf,srcd->fd", activated, branch_grad, preferred_element_type=jnp.float32
    )
    down_bias_local = jnp.sum(branch_grad.astype(jnp.float32), (0, 1, 2))
    act_grad = jnp.einsum(
        "srcd,fd->srcf", branch_grad, down_full, preferred_element_type=jnp.float32
    )
    unused_value, gelu_back = jax.vjp(gelu_exact, raised)
    raised_grad = gelu_back(act_grad)[0].astype(jnp.bfloat16)
    up_local = jnp.einsum(
        "srcd,srcf->df", second_norm, raised_grad, preferred_element_type=jnp.float32
    )
    up_bias_local = jnp.sum(raised_grad.astype(jnp.float32), (0, 1, 2))
    norm_grad = jnp.einsum(
        "srcf,df->srcd", raised_grad, up_full, preferred_element_type=jnp.float32
    )
    unused_value, second_back = jax.vjp(layer_norm, first_sum, second_gain, second_shift)
    sum_part, second_gain_local, second_shift_local = second_back(norm_grad)
    first_grad = second_grad + sum_part
    attn_grad = first_grad.astype(jnp.bfloat16)
    output_local = jnp.einsum(
        "srcd,srce->de", combined_own, attn_grad, preferred_element_type=jnp.float32
    )
    output_bias_local = jnp.sum(attn_grad.astype(jnp.float32), (0, 1, 2))
    mixed_grad = jnp.einsum(
        "srce,de->srcd", attn_grad, output_full, preferred_element_type=jnp.float32
    ).astype(jnp.bfloat16)
    grad_above = from_behind(mixed_grad[:, grid_rows - half_win :], "rows", 1)
    framed_grad = jnp.roll(
        jnp.concatenate([grad_above, mixed_grad[:, : grid_rows - half_win]], 1), half_win, 2
    )
    mixed_windows = to_windows(framed_grad).reshape(window_count, WIN * WIN, head_count, head_size)
    probs = jnp.exp(window_scores(queries, key_part, pos_bias, score_mask, score_scale) - log_total)
    prob_grad = jnp.einsum(
        "wqhe,wkhe->whqk", mixed_windows, value_part, preferred_element_type=jnp.float32
    )
    value_grad = jnp.einsum(
        "whqk,wqhe->wkhe",
        probs.astype(jnp.bfloat16),
        mixed_windows,
        preferred_element_type=jnp.float32,
    )
    score_grad = (probs * (prob_grad - jnp.sum(prob_grad * probs, -1, keepdims=True))).astype(
        jnp.bfloat16
    )
    pair_grad = jnp.sum(score_grad.astype(jnp.float32), 0).reshape(head_count, -1).T
    table_local = jnp.dot(onehot.T, pair_grad, precision=HIGHEST)
    query_grad = (
        jnp.einsum("whqk,wkhe->wqhe", score_grad, key_part, preferred_element_type=jnp.float32)
        * score_scale
    )
    key_grad = (
        jnp.einsum("whqk,wqhe->wkhe", score_grad, queries, preferred_element_type=jnp.float32)
        * score_scale
    )
    qkv_grad = jnp.concatenate(
        [
            query_grad.reshape(window_count, WIN * WIN, model_width),
            key_grad.reshape(window_count, WIN * WIN, model_width),
            value_grad.reshape(window_count, WIN * WIN, model_width),
        ],
        -1,
    ).astype(jnp.bfloat16)
    qkv_local = jnp.einsum("wtd,wtf->df", windowed, qkv_grad, preferred_element_type=jnp.float32)
    framed_norm = jnp.einsum("wtf,df->wtd", qkv_grad, qkv_full, preferred_element_type=jnp.float32)
    framed_norm = jnp.roll(from_windows(framed_norm, samples, grid_rows, grid_cols), -half_win, 2)
    from_next = from_behind(framed_norm[:, :half_win].astype(jnp.bfloat16), "rows", -1).astype(
        jnp.float32
    )
    normed_grad = jnp.concatenate([framed_norm[:, half_win:], from_next], 1)
    unused_value, first_back = jax.vjp(layer_norm, inputs, first_gain, first_shift)
    input_part, first_gain_local, first_shift_local = first_back(normed_grad)
    input_grad = first_grad + input_part
    qkv_weight_grad, output_weight_grad, up_weight_grad, down_weight_grad, conv_weight_grad = (
        lax.psum_scatter(qkv_local, ("rows", "batch"), scatter_dimension=0, tiled=True),
        lax.psum_scatter(output_local, ("rows", "batch"), scatter_dimension=0, tiled=True),
        lax.psum_scatter(up_local, ("rows", "batch"), scatter_dimension=0, tiled=True),
        lax.psum_scatter(down_local, ("rows", "batch"), scatter_dimension=0, tiled=True),
        lax.psum_scatter(conv_local, ("rows", "batch"), scatter_dimension=0, tiled=True),
    )
    (
        first_gain_grad,
        first_shift_grad,
        bias_table_grad,
        output_bias_grad,
        second_gain_grad,
        second_shift_grad,
        up_bias_grad,
        down_bias_grad,
        conv_bias_grad,
    ) = lax.psum(
        (
            first_gain_local,
            first_shift_local,
            table_local,
            output_bias_local,
            second_gain_local,
            second_shift_local,
            up_bias_local,
            down_bias_local,
            conv_bias_local,
        ),
        ("rows", "batch"),
    )
    return (
        layer_output,
        input_grad,
        hidden_grad,
        first_gain_grad,
        first_shift_grad,
        qkv_weight_grad,
        bias_table_grad,
        output_weight_grad,
        output_bias_grad,
        second_gain_grad,
        second_shift_grad,
        up_weight_grad,
        up_bias_grad,
        down_weight_grad,
        down_bias_grad,
        conv_weight_grad,
        conv_bias_grad,
    )


def solution(mesh):
    in_specs = (
        P("batch", "rows", None, None),
        P("batch", "rows", None, None),
        P("batch"),
        P("batch"),
        P(),
        P(),
        P(("rows", "batch"), None),
        P(),
        P(("rows", "batch"), None),
        P(),
        P(),
        P(),
        P(("rows", "batch"), None),
        P(),
        P(("rows", "batch"), None),
        P(),
        P(("rows", "batch"), None),
        P(),
        P("batch", "rows", None, None),
    )
    out_specs = (
        P("batch", "rows", None, None),
        P("batch", "rows", None, None),
        P("batch", "rows", None, None),
        P(),
        P(),
        P(("rows", "batch"), None),
        P(),
        P(("rows", "batch"), None),
        P(),
        P(),
        P(),
        P(("rows", "batch"), None),
        P(),
        P(("rows", "batch"), None),
        P(),
        P(("rows", "batch"), None),
        P(),
    )
    return jax.shard_map(shards, mesh=mesh, in_specs=in_specs, out_specs=out_specs, check_vma=False)
```

profile of v0, /device:TPU:0, one launch (start us, length us, event | category | flops | bytes accessed | tf_op | source)
XLA Modules:
  0.0 1232.8 jit_solution(2828878818846701965)
XLA Ops:
  24.4 5.2 collective-permute-start.4
  36.3 70.6 %all_gather.20 = bf16[256,768]{1,0:T(8,128)(2,1)S(1)} all-gather(bf16[8,768]{1,0:T(8,128)(2,1)S(1)} %convert_element_type.130), channel_id=1, replica_groups=mesh['rows'=8,'batch'=4] {'rows','batch'}, dimensions={0}, use_global_device_ids=true | all-gather | bytes 405504 | tf_op jit(solution)/shard_map/all_gather | solution.py:128
  118.7 4.8 copy.175
  123.5 4.7 copy.174
  128.3 5.2 copy.173
  133.5 14.8 %fusion.232 = (f32[64,8,64]{2,1,0:T(8,128)S(1)}, f32[64,8,64,64]{2,3,1,0:T(8,128)}) fusion(f32[64,64,64]{1,2,0:T(8,128)} %select_add_fusion, f32[8,64,64]{1,2,0:T(8,128)S(1)} %bitcast.244, bf16[64,64,8,32]{1,3,2,0:T(8,128)(2,1)} %bitcast.226, bf16[64,64,8,32]{1,3,2,0:T(8,128)(2,1)} %bitcast.224), kind=kOutput, calls=%fused_computation.289 | convolution fusion | flops 142573568 | bytes 13893632 | tf_op jit(solution)/shard_map/wqhe,wkhe->whqk/dot_general | solution.py:67
  148.3 11.1 exponential_reduce_fusion
  160.1 11.6 convert_bitcast_fusion
  171.7 8.9 copy.181
  180.7 10.8 reshape_reshape.6
  194.8 73.1 %all_gather.23 = bf16[1024,256]{1,0:T(8,128)(2,1)} all-gather(bf16[32,256]{1,0:T(8,128)(2,1)S(1)} %convert_element_type.141), channel_id=1, replica_groups=mesh['rows'=8,'batch'=4] {'rows','batch'}, dimensions={0}, use_global_device_ids=true | all-gather | bytes 540672 | tf_op jit(solution)/shard_map/all_gather | solution.py:131
  268.5 66.4 %all_gather.21 = bf16[256,256]{1,0:T(8,128)(2,1)S(1)} all-gather(bf16[8,256]{1,0:T(8,128)(2,1)S(1)} %convert_element_type.137), channel_id=1, replica_groups=mesh['rows'=8,'batch'=4] {'rows','batch'}, dimensions={0}, use_global_device_ids=true | all-gather | bytes 135168 | tf_op jit(solution)/shard_map/all_gather | solution.py:129
  334.8 73.3 %all_gather.22 = bf16[256,1024]{1,0:T(8,128)(2,1)} all-gather(bf16[8,1024]{1,0:T(8,128)(2,1)S(1)} %convert_element_type.139), channel_id=1, replica_groups=mesh['rows'=8,'batch'=4] {'rows','batch'}, dimensions={0}, use_global_device_ids=true | all-gather | bytes 540672 | tf_op jit(solution)/shard_map/all_gather | solution.py:130
  411.0 7.4 fusion.14
  418.5 39.7 %multiply_convert_fusion.1 = (bf16[2,16,128,1024]{3,2,1,0:T(8,128)(2,1)}, f32[2,16,128,1024]{3,2,1,0:T(8,128)}) fusion(f32[2,16,128,1024]{3,2,1,0:T(8,128)S(1)} %get-tuple-element.68, f32[1024]{0:T(1024)S(1)} %copy-done.67, u16[2,128,1024]{2,1,0:T(8,128)(2,1)S(1)} %get-tuple-element.18, u16[2,128,1024]{2,1,0:T(8,128)(2,1)S(1)} %get-tuple-element.17), kind=kLoop, calls=%fused_computation.12 | loop fusion | flops 297795584 | bytes 42995712 | tf_op jit(solution)/shard_map/convert_element_type | solution.py:178
  458.3 6.2 add_add_fusion.5
  473.9 4.9 fusion.23
  478.8 17.4 %fusion.229 = (bf16[2,16,128,512]{3,2,1,0:T(8,128)(2,1)}, bf16[2,16,128,512]{3,2,1,0:T(8,128)(2,1)}, bf16[2,16,128,512]{3,2,1,0:T(8,128)(2,1)}, bf16[2,16,128,51...) fusion(bf16[2,18,130,512]{3,2,1,0:T(8,128)(2,1)} %fusion.23), kind=kLoop, calls=%fused_computation.286 | loop fusion | bytes 50331648 | tf_op jit(solution)/shard_map/slice | solution.py:193
  496.1 5.0 fusion.118
  501.1 6.2 fusion.73
  511.9 4.6 fusion.82
  516.5 4.6 fusion.84
  521.1 4.6 fusion.86
  525.8 4.6 fusion.88
  534.9 4.6 fusion.187
  539.5 21.7 %add_multiply_fusion = f32[2,16,128,512]{3,2,1,0:T(8,128)S(1)} fusion(f32[2,16,128,512]{3,2,1,0:T(8,128)} %fusion.73, f32[2,16,128,512]{3,2,1,0:T(8,128)} %fusion.82, f32[2,16,128,512]{3,2,1,0:T(8,128)} %fusion.84, f32[2,16,128,512]{3,2,1,0:T(8,128)} %fusion.187, f32[2,16,128,512]{3,2,1,0:T(8,128)} %fusion.86, f32[2,16,128,512]{3,2,1,0:T(8,128)} %fusion.88, ...), kind=kOutput, calls=%fused_computation.40 | convolution fusion | flops 1092616192 | bytes 77873152 | tf_op jit(solution)/shard_map/srcy,xy->srcx/dot_general | solution.py:219
  565.9 18.0 %convert_reduce_fusion = (f32[1024]{0:T(1024)}, bf16[2,16,128,1024]{3,2,1,0:T(8,128)(2,1)}) fusion(f32[2,16,128,1024]{3,2,1,0:T(8,128)} %get-tuple-element.46, bf16[2,16,128,256]{3,2,1,0:T(8,128)(2,1)S(1)} %get-tuple-element.36, bf16[1024,256]{1,0:T(8,128)(2,1)} %all_gather.23, f32[2,16,128,1024]{3,2,1,0:T(8,128)} %copy-done.19, f32[1024]{0:T(1024)S(1)} %copy-done.67), kind=kOutput, calls=%fused_computation.7 | convolution fusion | flops 2218785792 | bytes 44572672 | tf_op jit(solution)/shard_map/srcd,fd->srcf/dot_general | solution.py:241
  583.9 7.1 multiply_reduce_fusion.1
  610.6 10.4 reshape_reshape.7
  621.0 9.1 copy.184
  630.1 10.7 convolution_convert_fusion.1
  640.9 14.3 %multiply_reduce_fusion = (f32[64,8,64]{2,1,0:T(8,128)S(1)}, f32[64,8,64,64]{2,3,1,0:T(8,128)}) fusion(f32[64,8,64,64]{2,3,1,0:T(8,128)} %get-tuple-element.65, f32[64,8,64]{2,1,0:T(8,128)S(1)} %copy-done.23, bf16[64,64,8,32]{1,3,2,0:T(8,128)(2,1)} %copy.184, bf16[64,64,8,32]{1,3,2,0:T(8,128)(2,1)} %bitcast.229), kind=kOutput, calls=%fused_computation.10 | convolution fusion | flops 140476416 | bytes 21233664 | tf_op jit(solution)/shard_map/wqhe,wkhe->whqk/dot_general | solution.py:270
  655.2 16.4 %convert_reduce_fusion.1 = (f32[8,64,64]{1,2,0:T(8,128)}, bf16[64,8,64,64]{2,3,1,0:T(8,128)(2,1)}) fusion(f32[64,8,64,64]{2,3,1,0:T(8,128)} %get-tuple-element.71, f32[64,8,64]{2,1,0:T(8,128)S(1)} %get-tuple-element.70, f32[64,8,64,64]{2,3,1,0:T(8,128)} %get-tuple-element.65, f32[64,8,64]{2,1,0:T(8,128)S(1)} %copy-done.23), kind=kLoop, calls=%fused_computation.8 | loop fusion | flops 12550144 | bytes 21364736 | tf_op jit(solution)/shard_map/reduce_sum | solution.py:282
  671.6 11.2 multiply_convert_fusion.2
  682.8 9.0 multiply_convert_fusion.3
  691.8 4.8 copy.191
  696.5 4.8 copy.189
  701.3 4.8 copy.190
  706.1 6.2 fusion.114
  716.8 6.8 fusion.108
  730.3 7.5 fusion.103
  750.9 5.5 fusion.31
  786.2 13.7 %multiply_convert_fusion.5 = bf16[2,16,128,256]{3,2,1,0:T(8,128)(2,1)} fusion(f32[2,16,128,256]{3,2,1,0:T(8,128)} %fusion.31, f32[2,16,128,256]{3,2,1,0:T(8,128)} %fusion.190, f32[2,16,128,256]{3,2,1,0:T(8,128)} %fusion.189, f32[2,16,128,256]{3,2,1,0:T(8,128)} %fusion.188, f32[2,16,128,256]{3,2,1,0:T(8,128)} %fusion.186, f32[2,16,128,256]{3,2,1,0:T(8,128)} %fusion.185, ...), kind=kOutput, calls=%fused_computation.108 | convolution fusion | flops 1085276160 | bytes 40125440 | tf_op jit(solution)/shard_map/srcx,xy->srcy/dot_general | solution.py:194
  812.4 48.5 %all-reduce.2 = (f32[256]{0:T(256)}, f32[256]{0:T(256)}, f32[225,8]{0,1:T(8,128)}, f32[256]{0:T(256)}, f32[256]{0:T(256)}, /*index=5*/f32[256]{0:T(256)}, f32[1024]{0:T(1024)}, f32[256]{0:T(256)}, f32[256]{0:T(256)}) all-reduce(f32[256]{0:T(256)S(1)} %get-tuple-element.21, ...), channel_id=1, replica_groups=mesh['rows'=8,'batch'=4] {'rows','batch'}, use_global_device_ids=true, to_apply=%region_12.13 | all-reduce | flops 4616 | bytes 36928 | tf_op jit(solution)/shard_map/psum | solution.py:327
  860.9 10.0 fusion.227
  870.9 109.7 %reduce-scatter.12.cloned.1.call-done = f32[32,256]{1,0:T(8,128)} async-done(((f32[1024,256]{1,0:T(8,128)}), f32[32,256]{1,0:T(8,128)}) %reduce-scatter.12.cloned.1.call-update) | async-done | bytes 32784 | tf_op jit(solution)/shard_map/reduce_scatter | solution.py:314
  980.7 134.6 %reduce-scatter.10.cloned.1.call-done = f32[8,1024]{1,0:T(8,128)} async-done(((f32[256,1024]{1,0:T(8,128)}), f32[8,1024]{1,0:T(8,128)}) %reduce-scatter.10.cloned.1.call-update) | async-done | bytes 32784 | tf_op jit(solution)/shard_map/reduce_scatter | solution.py:313
  1115.3 110.5 %reduce-scatter.14.cloned.1.call-done = f32[144,256]{1,0:T(8,128)} async-done(((f32[4608,256]{1,0:T(8,128)}), f32[144,256]{1,0:T(8,128)}) %reduce-scatter.14.cloned.1.call-update) | async-done | bytes 147472 | tf_op jit(solution)/shard_map/reduce_scatter | solution.py:315
  (301 shorter events, 151.6 us)
Async XLA Ops:
  7.2 22.9 %copy-start = (f32[225,8]{0,1:T(8,128)S(1)}, f32[225,8]{0,1:T(8,128)}, u32[]{:S(2)}) copy-start(f32[225,8]{0,1:T(8,128)} %param.26) | copy-start | bytes 21604
  7.2 7.2 copy-start.2
  7.2 7.2 copy-start.64
  7.2 7.2 copy-start.77
  7.2 493.9 %all-gather.2.cloned.1.call-start = ((), (), s32[]{:S(2)}) async-start(), calls=%async_computation.5 | async-start | bytes 2433024 | tf_op jit(solution)/shard_map/all_gather | solution.py:132
  9.0 861.9 %reduce-scatter.8.cloned.1.call-start = ((), (), s32[]{:S(2)}) async-start(), calls=%async_computation.7 | async-start | bytes 270336 | tf_op jit(solution)/shard_map/reduce_scatter | solution.py:312
  11.3 7.1 copy-start.78
  11.3 7.2 copy-start.79
  11.3 6.6 copy-start.44
  17.9 91.7 %collective-permute-start = (bf16[2,4,128,256]{3,2,1,0:T(8,128)(2,1)}, bf16[2,4,128,256]{3,2,1,0:T(8,128)(2,1)}, u32[]{:S(2)}, u32[]{:S(2)}) collective-permute-start(bf16[2,4,128,256]{3,2,1,0:T(8,128)(2,1)} %slice.237), channel_id=1, source_target_pairs={{0,4},{4,8},{8,12},{12,16},{16,20},{20,24},{24,28},{28,0},{1,5},{5... | collective-permute-start | bytes 1572872 | tf_op jit(solution)/shard_map/ppermute | solution.py:16
  18.6 520.8 %copy-start.51 = (f32[2,16,128]{2,1,0:T(8,128)}, f32[2,16,128]{2,1,0:T(8,128)S(1)}, u32[]{:S(2)}) copy-start(f32[2,16,128]{2,1,0:T(8,128)S(1)} %and_convert_fusion.3) | copy-start | bytes 49156
  18.6 17.0 %copy-start.61 = (f32[8,768]{1,0:T(8,128)S(1)}, f32[8,768]{1,0:T(8,128)}, u32[]{:S(2)}) copy-start(f32[8,768]{1,0:T(8,128)} %param.25) | copy-start | bytes 73732
  18.6 17.0 %copy-start.59 = (f32[32,256]{1,0:T(8,128)S(1)}, f32[32,256]{1,0:T(8,128)}, u32[]{:S(2)}) copy-start(f32[32,256]{1,0:T(8,128)} %param.33) | copy-start | bytes 98308
  23.2 444.9 %collective-permute-start.5 = (bf16[2,1,128,256]{3,2,1,0:T(8,128)(2,1)}, bf16[2,1,128,256]{3,2,1,0:T(8,128)(2,1)S(1)}, u32[]{:S(2)}, u32[]{:S(2)}) collective-permute-start(bf16[2,1,128,256]{3,2,1,0:T(8,128)(2,1)} %get-tuple-element.62), channel_id=1, source_target_pairs={{4,0},{8,4},{12,8},{16,12},{20,16},{24,20},{28,24},{5,1},{9,5},{13... | collective-permute-start | bytes 393224 | tf_op jit(solution)/shard_map/ppermute | solution.py:27
  24.4 443.7 %collective-permute-start.4 = (bf16[2,1,128,256]{3,2,1,0:T(8,128)(2,1)S(1)}, bf16[2,1,128,256]{3,2,1,0:T(8,128)(2,1)S(1)}, u32[]{:S(2)}, u32[]{:S(2)}) collective-permute-start(bf16[2,1,128,256]{3,2,1,0:T(8,128)(2,1)S(1)} %get-tuple-element.63), channel_id=1, source_target_pairs={{0,4},{4,8},{8,12},{12,16},{16,20},{20,24},{24,28},{1,5},{5,9},{9,... | collective-permute-start | bytes 393224 | tf_op jit(solution)/shard_map/ppermute | solution.py:26
  30.0 5.6 copy-start.62
  106.9 5.8 copy-start.38
  193.3 74.6 %copy-start.66 = (f32[8,256]{1,0:T(8,128)S(1)}, f32[8,256]{1,0:T(8,128)}, u32[]{:S(2)}) copy-start(f32[8,256]{1,0:T(8,128)} %param.27) | copy-start | bytes 24580
  193.3 74.6 %copy-start.60 = (f32[8,1024]{1,0:T(8,128)S(1)}, f32[8,1024]{1,0:T(8,128)}, u32[]{:S(2)}) copy-start(f32[8,1024]{1,0:T(8,128)} %param.31) | copy-start | bytes 98308
  193.3 74.6 %copy-start.32 = (bf16[2,16,128,256]{3,2,1,0:T(8,128)(2,1)S(1)}, bf16[2,16,128,256]{3,2,1,0:T(8,128)(2,1)}, u32[]{:S(2)}) copy-start(bf16[2,16,128,256]{3,2,1,0:T(8,128)(2,1)} %param.20) | copy-start | bytes 6291460
  194.7 213.6 %collective-permute-start.1 = (bf16[2,4,128,256]{3,2,1,0:T(8,128)(2,1)S(1)}, bf16[2,4,128,256]{3,2,1,0:T(8,128)(2,1)S(1)}, u32[]{:S(2)}, u32[]{:S(2)}) collective-permute-start(bf16[2,4,128,256]{3,2,1,0:T(8,128)(2,1)S(1)} %pad_maximum_fusion.14), channel_id=1, source_target_pairs={{0,28},{4,0},{8,4},{12,8},{16,12},{20,16},{24,20},{28,24},{1,29},{... | collective-permute-start | bytes 1572872 | tf_op jit(solution)/shard_map/ppermute | solution.py:16
  267.9 140.4 %copy-start.68 = (f32[256]{0:T(256)S(1)}, f32[256]{0:T(256)}, u32[]{:S(2)}) copy-start(f32[256]{0:T(256)} %param.28) | copy-start | bytes 3076
  409.6 48.6 %copy-start.14 = (f32[2,16,128,256]{3,2,1,0:T(8,128)}, f32[2,16,128,256]{3,2,1,0:T(8,128)S(1)}, u32[]{:S(2)}) copy-start(f32[2,16,128,256]{3,2,1,0:T(8,128)S(1)} %get-tuple-element.67) | copy-start | bytes 12582916
  418.5 39.8 %copy-start.19 = (f32[2,16,128,1024]{3,2,1,0:T(8,128)}, f32[2,16,128,1024]{3,2,1,0:T(8,128)S(1)}, u32[]{:S(2)}) copy-start(f32[2,16,128,1024]{3,2,1,0:T(8,128)S(1)} %get-tuple-element.68) | copy-start | bytes 50331652
  418.5 39.8 %copy-start.50 = (bf16[1024,256]{1,0:T(8,128)(2,1)S(1)}, bf16[1024,256]{1,0:T(8,128)(2,1)}, u32[]{:S(2)}) copy-start(bf16[1024,256]{1,0:T(8,128)(2,1)} %all_gather.23) | copy-start | bytes 1572868
  418.5 39.8 %copy-start.80 = (f32[256]{0:T(256)S(1)}, f32[256]{0:T(256)}, u32[]{:S(2)}) copy-start(f32[256]{0:T(256)} %param.34) | copy-start | bytes 3076
  465.4 8.5 copy-start.4
  465.5 3.7 collective-permute-start.2
  466.8 3.4 collective-permute-start.3
  501.1 6.2 copy-start.11
  501.1 6.2 copy-start.26
  565.9 18.1 %copy-start.36 = (bf16[2,16,128,256]{3,2,1,0:T(8,128)(2,1)}, bf16[2,16,128,256]{3,2,1,0:T(8,128)(2,1)S(1)}, u32[]{:S(2)}) copy-start(bf16[2,16,128,256]{3,2,1,0:T(8,128)(2,1)S(1)} %get-tuple-element.36) | copy-start | bytes 6291460
  565.9 18.1 %copy-start.49 = (bf16[256,1024]{1,0:T(8,128)(2,1)S(1)}, bf16[256,1024]{1,0:T(8,128)(2,1)}, u32[]{:S(2)}) copy-start(bf16[256,1024]{1,0:T(8,128)(2,1)} %all_gather.22) | copy-start | bytes 1572868
  583.9 7.1 copy-start.15
  596.6 9.6 collective-permute-start.6
  603.0 267.9 %reduce-scatter.6.cloned.1.call-start = ((), (), s32[]{:S(2)}) async-start(), calls=%async_computation.6 | async-start | bytes 811008 | tf_op jit(solution)/shard_map/reduce_scatter | solution.py:311
  621.0 9.1 copy-start.23
  712.3 268.4 %reduce-scatter.12.cloned.1.call-start = ((), (), s32[]{:S(2)}) async-start(), calls=%async_computation.9 | async-start | bytes 1081344 | tf_op jit(solution)/shard_map/reduce_scatter | solution.py:314
  723.6 391.7 %reduce-scatter.10.cloned.1.call-start = ((), (), s32[]{:S(2)}) async-start(), calls=%async_computation.8 | async-start | bytes 1081344 | tf_op jit(solution)/shard_map/reduce_scatter | solution.py:313
  737.8 487.9 %reduce-scatter.14.cloned.1.call-start = ((), (), s32[]{:S(2)}) async-start(), calls=%async_computation.10 | async-start | bytes 4866048 | tf_op jit(solution)/shard_map/reduce_scatter | solution.py:315
  747.1 12.5 %slice-start = ((s8[5013504]{0:T(1024)(128)(4,1)}), s8[819200]{0:T(1024)(128)(4,1)S(1)}, s32[]{:S(2)}) async-start(s8[5013504]{0:T(1024)(128)(4,1)} %bitcast.222), calls=%async_computation.11 | async-start | bytes 1638400
  750.8 8.8 slice-start.1
  786.1 18.9 %collective-permute-start.7 = (bf16[2,4,128,256]{3,2,1,0:T(8,128)(2,1)}, bf16[2,4,128,256]{3,2,1,0:T(8,128)(2,1)}, u32[]{:S(2)}, u32[]{:S(2)}) collective-permute-start(bf16[2,4,128,256]{3,2,1,0:T(8,128)(2,1)} %fusion.174), channel_id=1, source_target_pairs={{0,28},{4,0},{8,4},{12,8},{16,12},{20,16},{24,20},{28,24},{1,29},{... | collective-permute-start | bytes 1572872 | tf_op jit(solution)/shard_map/ppermute | solution.py:16
  801.1 6.4 copy-start.3
  801.1 6.4 copy-start.45
  801.1 6.4 copy-start.65
  809.1 51.8 %copy-start.56 = (f32[2,16,128]{2,1,0:T(8,128)S(1)}, f32[2,16,128]{2,1,0:T(8,128)}, u32[]{:S(2)}) copy-start(f32[2,16,128]{2,1,0:T(8,128)} %copy-done.55) | copy-start | bytes 49156
  860.9 364.9 %copy-start.1 = (f32[225,8]{0,1:T(8,128)S(1)}, f32[225,8]{0,1:T(8,128)}, u32[]{:S(2)}) copy-start(f32[225,8]{0,1:T(8,128)} %param.26) | copy-start | bytes 21604
  (51 other events, 142.8 us)
Sparse Core Ops, SparseCore 0:
  10.9 60.3 all-gather.1
  603.1 141.5 reduce-scatter.7
  751.2 92.2 reduce-scatter.5
  846.2 134.4 reduce-scatter.11
  983.3 131.9 reduce-scatter.9
  1122.1 103.6 reduce-scatter.13
where the time goes:
time: 1240 us; the launch traced here: 1230 us
  waiting for transfers between devices  359 us (29%)
  blocking collectives  332 us (27%)
  matrix products  273 us (22%)
  other arithmetic  125 us (10%)
  local copies, waits for them, and re-layouts  118 us (10%)
  between operations  15.5 us (1%)
    reduce_scatter x1, waiting for transfers between devices, shards(): lax.psum_scatter(up_local, ('rows', 'batch'), scatter_dimension=0, tiled=...  135 us
    reduce_scatter x1, waiting for transfers between devices, shards(): lax.psum_scatter(conv_local, ('rows', 'batch'), scatter_dimension=0, tile...  110 us
    reduce_scatter x1, waiting for transfers between devices, shards(): lax.psum_scatter(down_local, ('rows', 'batch'), scatter_dimension=0, tile...  110 us
    all_gather x1, blocking collectives, shards(): lax.all_gather(up_weight.astype(jnp.bfloat16), ('rows', 'batch'), axis=0,...  73.3 us
    all_gather x1, blocking collectives, shards(): lax.all_gather(down_weight.astype(jnp.bfloat16), ('rows', 'batch'), axis=...  73.1 us
    all_gather x1, blocking collectives, shards(): lax.all_gather(qkv_weight.astype(jnp.bfloat16), ('rows', 'batch'), axis=0...  70.6 us
    all_gather x1, blocking collectives, shards(): lax.all_gather(output_weight.astype(jnp.bfloat16), ('rows', 'batch'), axi...  66.4 us
    dot_general x9, matrix products, shards(): jnp.einsum('srcy,xy->srcx', grad_slice, conv_full[first_row:first_row + j...  60.1 us
  transfers between devices with their start and end apart: 14, of which 5 were waited for; matrix products, arithmetic and copies ran while one was open for 33% of the time, Pallas kernels for 0%

commit v1 on v0

v1 whole, which is shorter than its diff:
```python
import functools

import jax
import jax.numpy as jnp
import numpy as np
from jax import lax
from jax.experimental import pallas as pl
from jax.experimental.pallas import tpu as pltpu
from jax.sharding import PartitionSpec as P

WIN = 8
EPSILON = 1e-05
MASKED = -100.0
HIGHEST = lax.Precision.HIGHEST
AXES = ("rows", "batch")
BF = jnp.bfloat16
F32 = jnp.float32
VMEM_LIMIT = 56 * 1024 * 1024
LOG2E = 1.4426950408889634


def dot(left, right):
    return jnp.dot(left, right, preferred_element_type=F32)


def dot_nt(left, right):
    return lax.dot_general(left, right, (((1,), (1,)), ((), ())), preferred_element_type=F32)


def dot_tn(left, right):
    return lax.dot_general(left, right, (((0,), (0,)), ((), ())), preferred_element_type=F32)


def iota(shape, dim):
    return lax.broadcasted_iota(jnp.int32, shape, dim)


def device_index():
    return lax.axis_index("rows") * lax.axis_size("batch") + lax.axis_index("batch")


def device_count():
    return lax.axis_size("rows") * lax.axis_size("batch")


def stages():
    batch = lax.axis_size("batch")
    rows = lax.axis_size("rows")
    row_bits = [batch << k for k in range(rows.bit_length() - 1)]
    batch_bits = [1 << k for k in range(batch.bit_length() - 1)]
    groups = [row_bits[:1]]
    rest = row_bits[1:]
    groups += [rest[k : k + 2] for k in range(0, len(rest), 2)]
    groups += [batch_bits[k : k + 2] for k in range(0, len(batch_bits), 2)]
    return [g for g in groups if g]


def flips(group):
    masks = [0]
    for bit in group:
        masks = masks + [m | bit for m in masks]
    return masks


def swap(x, mask):
    devices = device_count()
    return lax.ppermute(x, AXES, [(i, i ^ mask) for i in range(devices)])


def gather_parts(x):
    held = x[None]
    places = [0]
    for group in stages()[::-1]:
        masks = flips(group)
        held = jnp.concatenate([held] + [swap(held, m) for m in masks[1:]], 0)
        places = [p ^ m for m in masks for p in places]
    order = np.zeros(len(places), np.int32)
    for place, mask in enumerate(places):
        order[mask] = place
    wanted = jnp.asarray(order)[jnp.arange(len(places)) ^ device_index()]
    return jnp.take(held, wanted, axis=0)


def scatter_sums(x):
    devices = device_count()
    me = device_index()
    bits = devices.bit_length() - 1
    held = x.reshape((2,) * bits + x.shape[1:])
    left = [1 << k for k in range(bits)][::-1]
    for group in stages():
        for bit in group:
            k = left.index(bit)
            left.pop(k)
            held = jnp.moveaxis(held, k, 0) if k else held
            held = held.reshape(held.shape)
            left.insert(0, bit)
        lead = left[: len(group)]
        left = left[len(group) :]
        count = 1 << len(group)
        flat = held.reshape((count,) + held.shape[len(group) :])
        mine = 0
        for k, bit in enumerate(lead):
            mine = mine + ((me // bit) % 2) * (1 << (len(lead) - 1 - k))
        total = lax.dynamic_index_in_dim(flat, mine, 0, False).astype(F32)
        for mask in flips(group)[1:]:
            local = sum((1 << (len(lead) - 1 - k)) for k, bit in enumerate(lead) if mask & bit)
            piece = lax.dynamic_index_in_dim(flat, mine ^ local, 0, False).astype(BF)
            total = total + swap(piece, mask).astype(F32)
        held = total
    return held


def sum_all(x):
    for group in stages():
        total = x
        for mask in flips(group)[1:]:
            total = total + swap(x, mask)
        x = total
    return x


def ring(x, by):
    devices = lax.axis_size("rows")
    return lax.ppermute(x, "rows", [(i, (i + by) % devices) for i in range(devices)])


def norm_parts(x):
    centred = x - jnp.mean(x, -1, keepdims=True)
    rstd = lax.rsqrt(jnp.mean(centred * centred, -1, keepdims=True) + EPSILON)
    return centred * rstd, rstd


def norm_back(dy, xhat, rstd, gain):
    scaled = dy * gain
    first = jnp.mean(scaled, -1, keepdims=True)
    second = jnp.mean(scaled * xhat, -1, keepdims=True)
    return (scaled - first - xhat * second) * rstd


def head_mask():
    rows, lanes = np.arange(256)[:, None], np.arange(256)[None, :]
    return (rows // 64 == (lanes % 128) // 32).astype(np.float32)


def pair_of(ref, pair, column):
    first = ref[pl.ds(pair * 128, 64), column : column + 128]
    second = ref[pl.ds(pair * 128 + 64, 64), column : column + 128]
    return jnp.concatenate([first, second], 1)


def blocks_of(ref, pair, column):
    first = ref[pl.ds(pair * 128, 64), column : column + 128]
    second = ref[pl.ds(pair * 128 + 64, 64), column : column + 128]
    nothing = jnp.zeros_like(first)
    return jnp.concatenate(
        [jnp.concatenate([first, nothing], 1), jnp.concatenate([nothing, second], 1)], 0
    )


def spread_heads(pair, mask):
    return jnp.concatenate([pair] * 4, 0) * mask


def attn_forward_body(
    height, scale, step_of, place, x_ref, gain, shift, weight, bias, mask,
    x_out, norm_out, xhat_out, rstd_out, qkv_out, prob_out, mix_out, xs,
):
    sample, band = step_of(pl.program_id(0))
    columns = x_ref.shape[2]

    def rows_in(r, _):
        x = pltpu.roll(x_ref[0, r].astype(F32), WIN // 2, 0)
        xs[:, r] = x.reshape(columns // WIN, WIN, 256)
        return 0

    lax.fori_loop(0, WIN, rows_in, 0)

    def norm_in(k, _):
        tokens = pl.ds(k * 128, 128)
        x = xs[pl.ds(k * 2, 2)].reshape(128, 256)
        xhat, rstd = norm_parts(x)
        x_out[tokens] = x.astype(BF)
        xhat_out[tokens] = xhat
        rstd_out[tokens] = jnp.broadcast_to(rstd, (128, 128))
        norm_out[tokens] = (xhat * gain[...] + shift[...]).astype(BF)
        return 0

    lax.fori_loop(0, columns // 16, norm_in, 0)
    for k in range(0, columns * WIN, 256):
        qkv_out[k : k + 256] = dot(norm_out[k : k + 256], weight[...]).astype(BF)

    key_at, query_at = iota((64, 128), 0), iota((64, 128), 1)
    window_at = query_at // 64
    query_at = query_at % 64
    row_base = place[0] + band * WIN
    key_row, query_row = key_at // WIN + row_base, query_at // WIN + row_base
    key_row = jnp.where(key_row < 0, key_row + height, key_row)
    query_row = jnp.where(query_row < 0, query_row + height, query_row)
    rows_differ = (key_row >= height - WIN // 2) != (query_row >= height - WIN // 2)
    row_bad = key_row >= place[1 + sample]

    def attend(pair, _):
        key_col = (pair * 2 + window_at) * WIN + key_at % WIN - WIN // 2
        query_col = (pair * 2 + window_at) * WIN + query_at % WIN - WIN // 2
        key_col = jnp.where(key_col < 0, key_col + columns, key_col)
        query_col = jnp.where(query_col < 0, query_col + columns, query_col)
        cols_differ = (key_col >= columns - WIN // 2) != (query_col >= columns - WIN // 2)
        bad = row_bad | (key_col >= place[3 + sample])
        minus = jnp.where(rows_differ | cols_differ, MASKED / scale, 0.0) + jnp.where(
            bad, MASKED / scale, 0.0
        )
        for half in range(2):
            keys = spread_heads(pair_of(qkv_out, pair, 256 + 128 * half), mask[...])
            queries = blocks_of(qkv_out, pair, 128 * half)
            scores = dot_nt(keys, queries).reshape(4, 64, 128)
            scores = scores + (bias[256 * half : 256 * half + 256].reshape(4, 64, 128) + minus[None])
            top = jnp.max(scores, 1, keepdims=True)
            raised = jnp.exp2((scores - top) * (scale * LOG2E))
            probs = raised * (1.0 / jnp.sum(raised, 1, keepdims=True))
            probs = probs.reshape(256, 128).astype(BF)
            prob_out[pair, 256 * half : 256 * half + 256] = probs
            values = spread_heads(pair_of(qkv_out, pair, 512 + 128 * half), mask[...])
            mixed = dot_tn(probs, values).astype(BF)
            mix_out[pl.ds(pair * 128, 64), 128 * half : 128 * half + 128] = mixed[:64, :128]
            mix_out[pl.ds(pair * 128 + 64, 64), 128 * half : 128 * half + 128] = mixed[64:, 128:]
        return 0

    lax.fori_loop(0, columns // 16, attend, 0, unroll=2)


def const_spec(shape):
    return pl.BlockSpec(shape, lambda *_: (0,) * len(shape))


def params():
    return pltpu.CompilerParams(vmem_limit_bytes=VMEM_LIMIT)


SMEM_SPEC = pl.BlockSpec(memory_space=pltpu.SMEM)


def band_steps(samples, bands):
    def step_of(step):
        return step % samples, bands[0] + step // samples

    return step_of, samples * len(bands)


def attn_forward(place, framed, gain, shift, weight, bias, mask, height, scale):
    samples, grid_rows, columns, width = framed.shape
    bands = grid_rows // WIN
    tokens = WIN * columns
    steps = samples * bands

    def step_of(step):
        return step // bands, step % bands

    def row_block(step):
        return (step, 0)

    total = steps * tokens
    cost = pl.CostEstimate(flops=9 * 10**9, bytes_accessed=30 * 10**6, transcendentals=2 * 10**6)
    return pl.pallas_call(
        functools.partial(attn_forward_body, height, scale, step_of),
        grid=(steps,),
        in_specs=[
            SMEM_SPEC,
            pl.BlockSpec((1, WIN, columns, width), lambda s: (*step_of(s), 0, 0)),
            const_spec((1, width)),
            const_spec((1, width)),
            const_spec(weight.shape),
            const_spec(bias.shape),
            const_spec(mask.shape),
        ],
        out_specs=[
            pl.BlockSpec((tokens, width), row_block),
            pl.BlockSpec((tokens, width), row_block),
            pl.BlockSpec((tokens, width), row_block),
            pl.BlockSpec((tokens, 128), row_block),
            pl.BlockSpec((tokens, 3 * width), row_block),
            pl.BlockSpec((columns // 16, 512, 128), lambda s: (s, 0, 0)),
            pl.BlockSpec((tokens, width), row_block),
        ],
        out_shape=[
            jax.ShapeDtypeStruct((total, width), BF),
            jax.ShapeDtypeStruct((total, width), BF),
            jax.ShapeDtypeStruct((total, width), F32),
            jax.ShapeDtypeStruct((total, 128), F32),
            jax.ShapeDtypeStruct((total, 3 * width), BF),
            jax.ShapeDtypeStruct((total // 128, 512, 128), BF),
            jax.ShapeDtypeStruct((total, width), BF),
        ],
        scratch_shapes=[pltpu.VMEM((columns // WIN, WIN, WIN, width), F32)],
        compiler_params=params(),
        cost_estimate=cost,
        name="attn_forward",
    )(place, framed, gain, shift, weight, bias, mask)


def gelu_parts(x):
    size = jnp.abs(x)
    near = 1.0 / (1.0 + (0.3275911 * 0.7071067811865476) * size)
    bell = jnp.exp2(x * x * (-0.5 * LOG2E))
    tail = (
        (
            (((0.5 * 1.061405429 * near - 0.5 * 1.453152027) * near + 0.5 * 1.421413741) * near)
            - 0.5 * 0.284496736
        )
        * near
        + 0.5 * 0.254829592
    ) * (near * bell)
    share = jnp.where(x > 0, 1.0 - tail, tail)
    return x * share, share + x * (bell * 0.3989422804014327)


def ffn_forward_body(
    height, step_of, place, x_ref, mix, out_w, out_b, gain, shift, up_w, up_b, down_w, down_b,
    norm_out, xhat_out, rstd_out, act_out, slope_out, sum_out, sums,
):
    sample, band = step_of(pl.program_id(0))
    columns = sum_out.shape[2]
    chunk = 256

    def part(k, _):
        tokens = pl.ds(k * chunk, chunk)
        first = x_ref[tokens].astype(F32) + dot(mix[tokens], out_w[...]) + out_b[...]
        xhat, rstd = norm_parts(first)
        normed = (xhat * gain[...] + shift[...]).astype(BF)
        norm_out[tokens] = normed
        xhat_out[tokens] = xhat
        rstd_out[tokens] = jnp.broadcast_to(rstd, (chunk, 128))
        for f in range(0, 1024, 256):
            raised = dot(normed, up_w[:, f : f + 256]) + up_b[:, f : f + 256]
            act, slope = gelu_parts(raised)
            act_out[tokens, f : f + 256] = act.astype(BF)
            slope_out[tokens, f : f + 256] = slope.astype(BF)
        second = first + dot(act_out[tokens], down_w[...]) + down_b[...]
        sums[pl.ds(k * (chunk // 64), chunk // 64)] = second.reshape(chunk // 64, WIN, WIN, 256)
        return 0

    lax.fori_loop(0, columns * WIN // chunk, part, 0)
    column = iota((columns, 1), 0)

    def rows_out(r, _):
        row = place[0] + band * WIN + r
        row = jnp.where(row < 0, row + height, row)
        limit = jnp.where(row < place[1 + sample], place[3 + sample], 0)
        back = pltpu.roll(sums[:, r].reshape(columns, 256), columns - WIN // 2, 0)
        sum_out[0, r] = jnp.where(column < limit, back, 0.0).astype(BF)
        return 0

    lax.fori_loop(0, WIN, rows_out, 0)


def ffn_forward(place, x, mix, out_w, out_b, gain, shift, up_w, up_b, down_w, down_b, height, shape):
    samples, grid_rows, columns, width = shape
    bands = grid_rows // WIN
    tokens = WIN * columns
    steps = samples * bands
    hidden = up_w.shape[1]
    total = steps * tokens

    def step_of(step):
        return step // bands, step % bands

    def row_block(step):
        return (step, 0)

    rows = [width, width, 128, hidden, hidden]
    types = [BF, F32, F32, BF, BF]
    cost = pl.CostEstimate(flops=15 * 10**9, bytes_accessed=32 * 10**6, transcendentals=8 * 10**6)
    return pl.pallas_call(
        functools.partial(ffn_forward_body, height, step_of),
        grid=(steps,),
        in_specs=[SMEM_SPEC]
        + [pl.BlockSpec((tokens, width), row_block)] * 2
        + [const_spec(a.shape) for a in (out_w, out_b, gain, shift, up_w, up_b, down_w, down_b)],
        out_specs=[pl.BlockSpec((tokens, n), row_block) for n in rows]
        + [pl.BlockSpec((1, WIN, columns, width), lambda s: (*step_of(s), 0, 0))],
        out_shape=[jax.ShapeDtypeStruct((total, n), t) for n, t in zip(rows, types)]
        + [jax.ShapeDtypeStruct(shape, BF)],
        scratch_shapes=[pltpu.VMEM((columns // WIN, WIN, WIN, width), F32)],
        compiler_params=params(),
        cost_estimate=cost,
        name="ffn_forward",
    )(place, x, mix, out_w, out_b, gain, shift, up_w, up_b, down_w, down_b)


def column_sum(x):
    return jnp.sum(x, 0, keepdims=True)


def ffn_backward_body(
    branch, act, slope, normed, xhat_ref, rstd_ref, mix, out_w, gain, up_w, down_w,
    first_out, mixed_out, down_acc, up_acc, out_acc, vec_acc, up_vec, raised_s,
):
    @pl.when(pl.program_id(0) == 0)
    def _():
        for ref in (down_acc, up_acc, out_acc, vec_acc, up_vec):
            ref[...] = jnp.zeros_like(ref)

    chunk = branch.shape[0]
    upper = branch[...]
    low = upper.astype(BF)
    for f in range(0, 1024, 256):
        raised = (dot_nt(low, down_w[f : f + 256]) * slope[:, f : f + 256].astype(F32)).astype(BF)
        raised_s[:, f : f + 256] = raised
        up_vec[0:1, f : f + 256] += column_sum(raised.astype(F32))
    low_t = low.T
    normed_t = normed[...].T
    for f in range(0, 1024, 256):
        down_acc[:, f : f + 256] += dot(low_t, act[:, f : f + 256])
        up_acc[:, f : f + 256] += dot(normed_t, raised_s[:, f : f + 256])
    dy = dot_nt(raised_s[...], up_w[...])
    xhat = xhat_ref[...]
    rstd = rstd_ref[...]
    rstd = jnp.concatenate([rstd, rstd], 1)
    first = upper + norm_back(dy, xhat, rstd, gain[...])
    first_out[...] = first
    attn = first.astype(BF)
    out_acc[...] += dot(mix[...].T, attn)
    mixed_out[...] = dot_nt(attn, out_w[...]).astype(BF)
    vec_acc[0:1] += column_sum(low.astype(F32))
    vec_acc[1:2] += column_sum(dy * xhat)
    vec_acc[2:3] += column_sum(dy)
    vec_acc[3:4] += column_sum(attn.astype(F32))


def ffn_backward(branch, act, slope, normed, xhat, rstd, mix, out_w, gain, up_w, down_w):
    total, width = branch.shape
    hidden = up_w.shape[1]
    chunk = 512
    steps = total // chunk

    def row_block(step):
        return (step, 0)

    cost = pl.CostEstimate(flops=19 * 10**9, bytes_accessed=40 * 10**6, transcendentals=0)
    return pl.pallas_call(
        ffn_backward_body,
        grid=(steps,),
        in_specs=[
            pl.BlockSpec((chunk, a.shape[1]), row_block)
            for a in (branch, act, slope, normed, xhat, rstd, mix)
        ]
        + [const_spec(a.shape) for a in (out_w, gain, up_w, down_w)],
        out_specs=[
            pl.BlockSpec((chunk, width), row_block),
            pl.BlockSpec((chunk, width), row_block),
            const_spec((width, hidden)),
            const_spec((width, hidden)),
            const_spec((width, width)),
            const_spec((8, width)),
            const_spec((8, hidden)),
        ],
        out_shape=[
            jax.ShapeDtypeStruct((total, width), F32),
            jax.ShapeDtypeStruct((total, width), BF),
            jax.ShapeDtypeStruct((width, hidden), F32),
            jax.ShapeDtypeStruct((width, hidden), F32),
            jax.ShapeDtypeStruct((width, width), F32),
            jax.ShapeDtypeStruct((8, width), F32),
            jax.ShapeDtypeStruct((8, hidden), F32),
        ],
        scratch_shapes=[pltpu.VMEM((chunk, hidden), BF)],
        compiler_params=params(),
        cost_estimate=cost,
        name="ffn_backward",
    )(branch, act, slope, normed, xhat, rstd, mix, out_w, gain, up_w, down_w)


def attn_backward_body(
    scale, mixed, qkv, prob, normed, xhat_ref, rstd_ref, first, weight, gain, mask,
    input_out, qkv_acc, table_acc, vec_acc, grads, sums,
):
    @pl.when(pl.program_id(0) == 0)
    def _():
        for ref in (qkv_acc, table_acc, vec_acc):
            ref[...] = jnp.zeros_like(ref)

    columns = input_out.shape[2]
    tokens = columns * WIN

    def attend(pair, _):
        head_at = mask[...]
        for half in range(2):
            lanes = slice(256 * half, 256 * half + 256)
            low = prob[pair, lanes]
            mixed_blocks = blocks_of(mixed, pair, 128 * half)
            values = spread_heads(pair_of(qkv, pair, 512 + 128 * half), head_at)
            prob_grad = dot_nt(values, mixed_blocks).reshape(4, 64, 128)
            probs = low.astype(F32).reshape(4, 64, 128)
            shared = jnp.sum(prob_grad * probs, 1, keepdims=True)
            score_grad = (probs * (prob_grad - shared)).astype(BF).reshape(256, 128)
            table_acc[lanes] += score_grad.astype(F32)
            keys = spread_heads(pair_of(qkv, pair, 256 + 128 * half), head_at)
            queries = blocks_of(qkv, pair, 128 * half)
            query_grad = (dot_tn(score_grad, keys) * scale).astype(BF)
            out = slice(128 * half, 128 * half + 128)
            grads[pl.ds(pair * 128, 64), out] = query_grad[:64, :128]
            grads[pl.ds(pair * 128 + 64, 64), out] = query_grad[64:, 128:]
            wide = head_at.astype(F32)
            key_grad = (dot(score_grad, queries) * wide).reshape(4, 64, 256)
            key_grad = (jnp.sum(key_grad, 0) * scale).astype(BF)
            out = slice(256 + 128 * half, 256 + 128 * half + 128)
            grads[pl.ds(pair * 128, 64), out] = key_grad[:, :128]
            grads[pl.ds(pair * 128 + 64, 64), out] = key_grad[:, 128:]
            value_grad = (dot(low, mixed_blocks) * wide).reshape(4, 64, 256)
            value_grad = jnp.sum(value_grad, 0).astype(BF)
            out = slice(512 + 128 * half, 512 + 128 * half + 128)
            grads[pl.ds(pair * 128, 64), out] = value_grad[:, :128]
            grads[pl.ds(pair * 128 + 64, 64), out] = value_grad[:, 128:]
        return 0

    lax.fori_loop(0, columns // 16, attend, 0)
    for f in range(0, 768, 256):
        qkv_acc[:, f : f + 256] += dot_tn(normed[...], grads[:, f : f + 256])

    def part(k, _):
        at = pl.ds(k * 256, 256)
        dy = dot_nt(grads[at], weight[...])
        xhat = xhat_ref[at]
        rstd = rstd_ref[at]
        rstd = jnp.concatenate([rstd, rstd], 1)
        total = first[at] + norm_back(dy, xhat, rstd, gain[...])
        sums[pl.ds(k * 4, 4)] = total.reshape(4, WIN, WIN, 256)
        vec_acc[0:1] += column_sum(dy * xhat)
        vec_acc[1:2] += column_sum(dy)
        return 0

    lax.fori_loop(0, tokens // 256, part, 0)

    def rows_out(r, _):
        input_out[0, r] = pltpu.roll(sums[:, r].reshape(columns, 256), columns - WIN // 2, 0)
        return 0

    lax.fori_loop(0, WIN, rows_out, 0)


def attn_backward(mixed, qkv, prob, normed, xhat, rstd, first, weight, gain, mask, scale, shape, band):
    samples, grid_rows, columns, width = shape
    bands = grid_rows // WIN
    tokens = WIN * columns

    def row_block(step):
        return (step * bands + band, 0)

    cost = pl.CostEstimate(flops=8 * 10**9, bytes_accessed=16 * 10**6, transcendentals=0)
    return pl.pallas_call(
        functools.partial(attn_backward_body, scale),
        grid=(samples,),
        in_specs=[
            pl.BlockSpec((tokens, width), row_block),
            pl.BlockSpec((tokens, 3 * width), row_block),
            pl.BlockSpec((columns // 16, 512, 128), lambda s: (s * bands + band, 0, 0)),
            pl.BlockSpec((tokens, width), row_block),
            pl.BlockSpec((tokens, width), row_block),
            pl.BlockSpec((tokens, 128), row_block),
            pl.BlockSpec((tokens, width), row_block),
            const_spec(weight.shape),
            const_spec(gain.shape),
            const_spec(mask.shape),
        ],
        out_specs=[
            pl.BlockSpec((1, WIN, columns, width), lambda s: (s, 0, 0, 0)),
            const_spec((width, 3 * width)),
            const_spec((512, 128)),
            const_spec((8, width)),
        ],
        out_shape=[
            jax.ShapeDtypeStruct((samples, WIN, columns, width), F32),
            jax.ShapeDtypeStruct((width, 3 * width), F32),
            jax.ShapeDtypeStruct((512, 128), F32),
            jax.ShapeDtypeStruct((8, width), F32),
        ],
        scratch_shapes=[
            pltpu.VMEM((tokens, 3 * width), BF),
            pltpu.VMEM((columns // WIN, WIN, WIN, width), F32),
        ],
        compiler_params=params(),
        cost_estimate=cost,
        name="attn_backward",
    )(mixed, qkv, prob, normed, xhat, rstd, first, weight, gain, mask)


def shifted(row, column, by):
    columns = row.shape[0]
    moved = pltpu.roll(row, by % columns, 0)
    edge = 0 if by == 1 else columns - 1
    return jnp.where(column == edge, 0.0, moved)


def taps_in(source, target, rows, lanes):
    columns = source.shape[-2]
    column = iota((columns, 1), 0)

    def one(r, _):
        row = source[0, r]
        wide = row.astype(F32)
        target[r, :, lanes[0] : lanes[0] + 256] = shifted(wide, column, -1).astype(BF)
        target[r, :, lanes[1] : lanes[1] + 256] = row
        target[r, :, lanes[2] : lanes[2] + 256] = shifted(wide, column, 1).astype(BF)
        return 0

    lax.fori_loop(0, rows, one, 0)


def conv_weight_body(groups, joined, grad, acc, taps):
    @pl.when(pl.program_id(0) == 0)
    def _():
        acc[...] = jnp.zeros_like(acc)

    columns = joined.shape[2]
    taps_in(grad, taps, grad.shape[1], (0, 256, 512))
    for start, target, rows in groups:
        turned = joined[0, target : target + rows].reshape(rows * columns, 256).T
        for a in range(3):
            piece = taps[start + 2 - a : start + 2 - a + rows].reshape(rows * columns, 768)
            acc[a] += dot(turned, piece)


def conv_weight(groups, joined, grad):
    samples, rows, columns, width = joined.shape
    cost = pl.CostEstimate(flops=48 * 10**8, bytes_accessed=8 * 10**6, transcendentals=0)
    return pl.pallas_call(
        functools.partial(conv_weight_body, groups),
        grid=(samples,),
        in_specs=[
            pl.BlockSpec((1, rows, columns, width), lambda s: (s, 0, 0, 0)),
            pl.BlockSpec((1,) + grad.shape[1:], lambda s: (s, 0, 0, 0)),
        ],
        out_specs=const_spec((3, width, 3 * width)),
        out_shape=jax.ShapeDtypeStruct((3, width, 3 * width), F32),
        scratch_shapes=[pltpu.VMEM((grad.shape[1], columns, 3 * width), BF)],
        compiler_params=params(),
        cost_estimate=cost,
        name="conv_weight",
    )(joined, grad)


def conv_data_body(groups, height, framed, place, grad, weight, out, taps):
    sample = pl.program_id(0)
    columns = grad.shape[2]
    column = iota((columns, 1), 0)
    taps_in(grad, taps, grad.shape[1], (0, 256, 512))
    for start, target, rows in groups:
        for r in range(0, rows, 4):
            total = 0.0
            for a in range(3):
                first = start + r + 2 - a
                piece = taps[first : first + 4].reshape(4 * columns, 768)
                total = total + dot_nt(piece, weight[a])
            for k in range(4):
                at = target + r + k
                row = place[0] + at
                if framed:
                    row = jnp.where(row < 0, row + height, row)
                else:
                    row = row + WIN // 2
                limit = jnp.where(row < place[1 + sample], place[3 + sample], 0)
                part = jnp.where(column < limit, total[k * columns : (k + 1) * columns], 0.0)
                if framed:
                    part = pltpu.roll(part, WIN // 2, 0)
                    out[at // WIN, :, at % WIN] = part.reshape(columns // WIN, WIN, 256)
                else:
                    out[0, at] = part


def conv_data(groups, place, grad, weight, rows, height, framed):
    samples, _, columns, width = grad.shape
    if framed:
        shape = (samples * rows // WIN, columns // WIN, WIN, WIN, width)
        spec = pl.BlockSpec((rows // WIN,) + shape[1:], lambda s: (s, 0, 0, 0, 0))
    else:
        shape = (samples, rows, columns, width)
        spec = pl.BlockSpec((1,) + shape[1:], lambda s: (s, 0, 0, 0))
    cost = pl.CostEstimate(flops=48 * 10**8, bytes_accessed=8 * 10**6, transcendentals=0)
    return pl.pallas_call(
        functools.partial(conv_data_body, groups, height, framed),
        grid=(samples,),
        in_specs=[
            SMEM_SPEC,
            pl.BlockSpec((1,) + grad.shape[1:], lambda s: (s, 0, 0, 0)),
            const_spec(weight.shape),
        ],
        out_specs=spec,
        out_shape=jax.ShapeDtypeStruct(shape, F32),
        scratch_shapes=[pltpu.VMEM((grad.shape[1], columns, 3 * width), BF)],
        compiler_params=params(),
        cost_estimate=cost,
        name="conv_data",
    )(place, grad, weight)


def conv_forward_body(place, sums, hidden, weight, bias, out, taps):
    sample = pl.program_id(0)
    columns = sums.shape[2]
    rows = out.shape[1]
    column = iota((columns, 1), 0)
    taps_in(sums, taps, rows + 2, (1024, 512, 0))
    taps_in(hidden, taps, rows + 2, (1280, 768, 256))
    for r in range(0, rows, 4):
        total = bias[...]
        for a in range(3):
            piece = taps[r + a : r + a + 4].reshape(4 * columns, 1536)
            total = total + dot(piece, weight[a * 1536 : (a + 1) * 1536])
        for k in range(4):
            row = place[0] + WIN // 2 + r + k
            limit = jnp.where(row < place[1 + sample], place[3 + sample], 0)
            part = total[k * columns : (k + 1) * columns]
            out[0, r + k] = jnp.where(column < limit, part, 0.0).astype(BF)


def conv_forward(place, sums, hidden, weight, bias):
    samples, padded, columns, width = sums.shape
    rows = padded - 2
    cost = pl.CostEstimate(flops=96 * 10**8, bytes_accessed=10 * 10**6, transcendentals=0)
    return pl.pallas_call(
        conv_forward_body,
        grid=(samples,),
        in_specs=[
            SMEM_SPEC,
            pl.BlockSpec((1, padded, columns, width), lambda s: (s, 0, 0, 0)),
            pl.BlockSpec((1, padded, columns, width), lambda s: (s, 0, 0, 0)),
            const_spec(weight.shape),
            const_spec(bias.shape),
        ],
        out_specs=pl.BlockSpec((1, rows, columns, width), lambda s: (s, 0, 0, 0)),
        out_shape=jax.ShapeDtypeStruct((samples, rows, columns, width), BF),
        scratch_shapes=[pltpu.VMEM((padded, columns, 6 * width), BF)],
        compiler_params=params(),
        cost_estimate=cost,
        name="conv_forward",
    )(place, sums, hidden, weight, bias)


def offset_onehot():
    places = jnp.arange(WIN * WIN)
    row, col = places // WIN, places % WIN
    offsets = (row[None, :] - row[:, None] + WIN - 1) * (2 * WIN - 1) + (
        col[None, :] - col[:, None] + WIN - 1
    )
    return (offsets.reshape(-1)[:, None] == jnp.arange((2 * WIN - 1) ** 2)[None, :]).astype(F32)


def shards(
    layer_input,
    hidden_state,
    crop_rows,
    crop_cols,
    first_gain,
    first_shift,
    qkv_weight,
    bias_table,
    output_weight,
    output_bias,
    second_gain,
    second_shift,
    up_weight,
    up_bias,
    down_weight,
    down_bias,
    conv_weight_in,
    conv_bias,
    cotangent,
):
    samples, grid_rows, columns, width = layer_input.shape
    shape = layer_input.shape
    heads = bias_table.shape[1]
    scale = float((width // heads) ** (-0.5))
    half = WIN // 2
    devices = device_count()
    row_devices = lax.axis_size("rows")
    height = grid_rows * row_devices
    row_place = lax.axis_index("rows")
    row_start = row_place * grid_rows
    place = jnp.concatenate(
        [(row_start - half)[None].astype(jnp.int32), crop_rows, crop_cols]
    ).astype(jnp.int32)

    input_above = ring(layer_input[:, grid_rows - half :], 1)
    qkv_full = gather_parts(qkv_weight.astype(BF)).reshape(width, -1)
    grad_above = ring(cotangent[:, grid_rows - half - 1 :], 1)
    grad_below = ring(cotangent[:, :1], -1)
    hidden_above = ring(hidden_state[:, grid_rows - 1 :], 1)
    hidden_below = ring(hidden_state[:, :1], -1)
    mid = jnp.concatenate([output_weight, up_weight], 1).astype(BF)
    mid_full = gather_parts(mid).reshape(width, -1)
    output_full, up_full = mid_full[:, :width], mid_full[:, width:]
    tall = jnp.concatenate([down_weight, conv_weight_in], 0).astype(BF)
    down_rows = down_weight.shape[0]
    tall_full = gather_parts(tall)
    down_full = tall_full[:, :down_rows].reshape(-1, width)
    conv_full = tall_full[:, down_rows:].reshape(-1, width)
    conv_turned = (
        conv_full.reshape(3, 3, 2, width, width).transpose(2, 0, 3, 1, 4).reshape(2, 3, width, 3 * width)
    )

    first_device = row_place == 0
    last_device = row_place == row_devices - 1
    framed = jnp.concatenate([input_above, layer_input[:, : grid_rows - half]], 1)
    row_ids = jnp.concatenate(
        [jnp.arange(-half - 1, grid_rows + 1)]
    ) + row_start
    row_ids = row_ids % height
    valid = (row_ids[None, :, None] < crop_rows[:, None, None]) & (
        jnp.arange(columns)[None, None, :] < crop_cols[:, None, None]
    )
    zero = jnp.zeros((), BF)
    grad_all = jnp.concatenate([grad_above, cotangent, grad_below], 1)
    grad_all = jnp.where(valid[..., None], grad_all, zero)
    grad_first = jnp.where(first_device, zero, grad_all[:, half : half + 1])
    grad_zero = jnp.where(first_device, zero, grad_all[:, half + 1 : half + 2])
    grad_last = jnp.where(last_device, zero, grad_all[:, -1:])
    grad_frame = jnp.concatenate(
        [grad_all[:, : half + 1], grad_zero, grad_first, grad_all[:, half + 1 : grid_rows + 2]], 1
    )
    grad_own = jnp.concatenate([grad_first, grad_all[:, half + 1 : -1], grad_last], 1)
    hidden_all = jnp.concatenate([hidden_above, hidden_state, hidden_below], 1)
    own_valid = valid[:, half:]
    edge = jnp.arange(grid_rows + 2)
    inside = ~((edge == 0) & first_device) & ~((edge == grid_rows + 1) & last_device)
    own_valid = own_valid & inside[None, :, None]
    hidden_all = jnp.where(own_valid[..., None], hidden_all, zero)
    frame_groups = ((0, 0, half), (half + 2, half, grid_rows - half))
    own_groups = ((0, 0, grid_rows),)

    onehot = offset_onehot()
    pos_bias = jnp.dot(onehot, bias_table, precision=HIGHEST).reshape(WIN * WIN, WIN * WIN, heads)
    pos_bias = pos_bias.transpose(2, 0, 1).reshape(heads * WIN * WIN, WIN * WIN) * (1.0 / scale)
    pos_bias = jnp.concatenate([pos_bias, pos_bias], 1)
    mask = jnp.asarray(head_mask(), BF)

    def vec(v):
        return v.reshape(1, -1)

    conv_hidden = conv_weight(own_groups, hidden_all[:, 1:-1], grad_own)
    x, normed, xhat, rstd, qkv, prob, mix = attn_forward(
        place, framed, vec(first_gain), vec(first_shift), qkv_full, pos_bias, mask, height, scale
    )
    normed_2, xhat_2, rstd_2, act, slope, sums = ffn_forward(
        place, x, mix, output_full, vec(output_bias), vec(second_gain), vec(second_shift),
        up_full, vec(up_bias), down_full, vec(down_bias), height, shape,
    )
    sums_below = ring(sums[:, : half + 1], -1)
    branch = conv_data(frame_groups, place, grad_frame, conv_turned[0], grid_rows, height, True)
    branch = branch.reshape(-1, width)
    conv_sums = conv_weight(frame_groups, sums, grad_frame)
    first_grad, mixed, down_acc, up_acc, out_acc, vec_ffn, vec_up = ffn_backward(
        branch, act, slope, normed_2, xhat_2, rstd_2, mix, output_full, vec(second_gain),
        up_full, down_full,
    )
    conv_local = jnp.stack([conv_sums, conv_hidden], 0).astype(BF)
    conv_local = conv_local.reshape(2, 3, width, 3, width).transpose(1, 3, 0, 2, 4)
    conv_weight_grad = scatter_sums(conv_local.reshape(devices, -1, width))
    up_weight_grad = scatter_sums(up_acc.reshape(devices, -1, up_acc.shape[1]))
    down_weight_grad = scatter_sums(down_acc.T.reshape(devices, -1, width))
    output_weight_grad = scatter_sums(out_acc.reshape(devices, -1, width))

    back = functools.partial(
        attn_backward, mixed, qkv, prob, normed, xhat, rstd, first_grad, qkv_full,
        vec(first_gain), mask, scale, shape,
    )
    input_top, qkv_top, table_top, vec_top = back(0)
    input_from_below = ring(input_top[:, :half].astype(BF), -1).astype(F32)
    input_low, qkv_low, table_low, vec_low = back(1)
    qkv_acc = qkv_top + qkv_low
    table_acc = table_top + table_low
    vec_attn = vec_top + vec_low
    input_grad = jnp.concatenate([input_top[:, half:], input_low, input_from_below], 1)
    qkv_weight_grad = scatter_sums(qkv_acc.reshape(devices, -1, qkv_acc.shape[1]))
    pair_grad = (table_acc[:, :64] + table_acc[:, 64:]).reshape(heads, -1)
    table_local = jnp.dot(pair_grad, onehot, precision=HIGHEST).T
    conv_bias_local = jnp.sum(grad_own[:, 1:-1].astype(F32), (0, 1, 2))
    small = [
        vec_attn[0], vec_attn[1], table_local, vec_ffn[3], vec_ffn[1], vec_ffn[2], vec_up[0],
        vec_ffn[0], conv_bias_local,
    ]
    flat = jnp.concatenate([v.reshape(-1) for v in small])
    count = flat.shape[0]
    flat = jnp.pad(flat, (0, -count % 1024)).reshape(-1, 128)
    flat = sum_all(flat).reshape(-1)[:count]
    summed = []
    for v in small:
        summed.append(flat[: v.size].reshape(v.shape))
        flat = flat[v.size :]
    (
        first_gain_grad, first_shift_grad, bias_table_grad, output_bias_grad, second_gain_grad,
        second_shift_grad, up_bias_grad, down_bias_grad, conv_bias_grad,
    ) = summed

    hidden_grad = conv_data(own_groups, place, grad_own, conv_turned[1], grid_rows, height, False)
    sums_own = jnp.concatenate([sums[:, half - 1 :], sums_below], 1)
    sums_own = jnp.where(inside[None, :, None, None], sums_own, zero)
    layer_output = conv_forward(place, sums_own, hidden_all, conv_full, vec(conv_bias))
    return (
        layer_output,
        input_grad,
        hidden_grad,
        first_gain_grad,
        first_shift_grad,
        qkv_weight_grad,
        bias_table_grad,
        output_weight_grad,
        output_bias_grad,
        second_gain_grad,
        second_shift_grad,
        up_weight_grad,
        up_bias_grad,
        down_weight_grad,
        down_bias_grad,
        conv_weight_grad,
        conv_bias_grad,
    )


def solution(mesh):
    field = P("batch", "rows", None, None)
    weight = P(AXES, None)
    in_specs = (
        field, field, P("batch"), P("batch"), P(), P(), weight, P(), weight, P(), P(), P(),
        weight, P(), weight, P(), weight, P(), field,
    )
    out_specs = (
        field, field, field, P(), P(), weight, P(), weight, P(), P(), P(), weight, P(), weight,
        P(), weight, P(),
    )
    return jax.shard_map(shards, mesh=mesh, in_specs=in_specs, out_specs=out_specs, check_vma=False)
```

time: 1240 us -> 461 us (0.37)
  blocking collectives: 332 us -> 0 us
  waiting for transfers between devices: 359 us -> 47.6 us
  matrix products: 273 us -> 6.15 us
  Pallas kernels: 0 us -> 188 us
  other arithmetic: 125 us -> 49.8 us
  starting transfers between devices: 10.4 us -> 84.7 us
  local copies, waits for them, and re-layouts: 118 us -> 76.5 us
  between operations: 15.5 us -> 1.67 us
    reduce_scatter x5 -> x0, waiting for transfers between devices: 355 us -> none  [the longest x1 135 us: shards(): lax.psum_scatter(up_local, ('rows', 'batch'), scatter_dimension=0, tiled=...]
    all_gather x4 -> x0, blocking collectives: 283 us -> none  [the longest x1 73.3 us: shards(): lax.all_gather(up_weight.astype(jnp.bfloat16), ('rows', 'batch'), axis=0,...]
    dot_general x46 -> x1, matrix products: 270 us -> 3.3 us  [shards(): table_local = jnp.dot(pair_grad, onehot, precision=HIGHEST).T]
    pallas_call x0 -> x10, Pallas kernels: none -> 188 us  [the longest x2 47.2 us: attn_backward(): pl.pallas_call(functools.partial(attn_backward_body, scale), grid=(sample...]
    ppermute x8 -> x70, starting transfers between devices: 9.79 us -> 84.7 us  [the longest x63 81.5 us: swap(): return lax.ppermute(x, AXES, [(i, i ^ mask) for i in range(devices)])]
    reduce_sum x14 -> x1, other arithmetic: 50 us -> 1.13 us  [shards(): conv_bias_local = jnp.sum(grad_own[:, 1:-1].astype(F32), (0, 1, 2))]
    psum x1 -> x0, blocking collectives: 48.5 us -> none  [shards(): lax.psum((first_gain_local, first_shift_local, table_local, output_bias_l...]
    convert_element_type x12 -> x1, other arithmetic: 45.4 us -> 0.09 us  [shards(): input_from_below = ring(input_top[:, :half].astype(BF), -1).astype(F32)]
  transfers between devices with their start and end apart: 14 -> 70, of which waited for: 5 -> 22; matrix products, arithmetic and copies ran while one was open for 33% -> 22% of each run, Pallas kernels for 0% -> 13%
where the time goes in v1:
time: 461 us; the launch traced here: 454 us
  Pallas kernels  188 us (41%)
  starting transfers between devices  84.7 us (18%)
  local copies, waits for them, and re-layouts  76.5 us (17%)
  other arithmetic  49.8 us (11%)
  waiting for transfers between devices  47.6 us (10%)
  matrix products  6.15 us (1%)
    ppermute x63, starting transfers between devices, swap(): return lax.ppermute(x, AXES, [(i, i ^ mask) for i in range(devices)])  81.5 us
    pallas_call x2, Pallas kernels, attn_backward(): pl.pallas_call(functools.partial(attn_backward_body, scale), grid=(sample...  47.2 us
    ppermute x63, waiting for transfers between devices, swap(): return lax.ppermute(x, AXES, [(i, i ^ mask) for i in range(devices)])  45.8 us
    pallas_call x1, Pallas kernels, attn_forward(): pl.pallas_call(functools.partial(attn_forward_body, height, scale, step_o...  34.9 us
    pallas_call x1, Pallas kernels, ffn_forward(): pl.pallas_call(functools.partial(ffn_forward_body, height, step_of), grid...  30.7 us
    pallas_call x1, Pallas kernels, ffn_backward(): pl.pallas_call(ffn_backward_body, grid=(steps,), in_specs=[pl.BlockSpec((...  20.6 us
    unnamed x87, local copies, waits for them, and re-layouts  20.1 us
    pallas_call x2, Pallas kernels, conv_weight(): pl.pallas_call(functools.partial(conv_weight_body, groups), grid=(samples...  19.4 us
  transfers between devices with their start and end apart: 70, of which 22 were waited for; matrix products, arithmetic and copies ran while one was open for 22% of the time, Pallas kernels for 13%

profile of v1, /device:TPU:0, one launch (start us, length us, event | category | flops | bytes accessed | tf_op | source)
XLA Modules:
  0.0 454.3 jit_solution(11169987262900742143)
XLA Ops:
  2.0 5.0 %collective-permute-start.3 = (bf16[1,8,768]{2,1,0:T(8,128)(2,1)S(1)}, bf16[1,8,768]{2,1,0:T(8,128)(2,1)}, u32[]{:S(2)}, u32[]{:S(2)}) collective-permute-start(bf16[1,8,768]{2,1,0:T(8,128)(2,1)S(1)} %get-tuple-element.108), channel_id=1, source_target_pairs={{0,3},{1,2},{2,1},{3,0},{4,7},{5,6},{6,5},{7,4},{8,11},{9,10},{10,... | collective-permute-start | bytes 36872 | tf_op jit(solution)/shard_map/ppermute | solution.py:67
  9.7 2.4 collective-permute-start.9
  12.1 2.0 collective-permute-start.8
  20.3 2.9 convolution_multiply_fusion
  32.4 2.0 slice.173
  37.3 2.9 collective-permute-start.15
  58.4 2.6 collective-permute-done.6
  61.6 2.6 collective-permute-start.24
  67.7 2.4 collective-permute-done.11
  72.6 3.8 collective-permute-done.12
  78.8 3.0 collective-permute-done.13
  86.4 2.1 maximum_select_fusion.2.hidden
  96.7 7.3 %collective-permute-done.18 = bf16[4,176,256]{2,1,0:T(8,128)(2,1)S(1)} collective-permute-done((bf16[4,176,256]{2,1,0:T(8,128)(2,1)}, bf16[4,176,256]{2,1,0:T(8,128)(2,1)S(1)}, u32[]{:S(2)}, u32[]{:S(2)}) %collective-permute-start.18) | collective-permute-done | bytes 360480 | tf_op jit(solution)/shard_map/ppermute | solution.py:67
  110.7 2.5 pad_maximum_fusion.3.x_ref
  113.3 34.9 %attn_forward.1 = (bf16[4096,256]{1,0:T(8,128)(2,1)}, bf16[4096,256]{1,0:T(8,128)(2,1)}, f32[4096,256]{1,0:T(8,128)}, f32[4096,128]{1,0:T(8,128)}, bf16[4096,768...) custom-call(s32[5]{0:T(128)} %pad_add_fusion.place, ...), custom_call_target="tpu_custom_call" | custom-call | flops 8999999488 | bytes 30000000 | tf_op jit(solution)/shard_map/attn_forward/pallas_call | solution.py:263
  148.2 2.4 maximum_select_fusion
  155.2 9.6 %conv_weight.3 = f32[3,256,768]{2,1,0:T(8,128)} custom-call(bf16[2,16,128,256]{3,2,1,0:T(8,128)(2,1)} %slice.241.joined, bf16[2,18,128,256]{3,2,1,0:T(8,128)(2,1)} %pad_maximum_fusion.2.grad), custom_call_target="tpu_custom_call" | custom-call | flops 4800000000 | bytes 8000000 | tf_op jit(solution)/shard_map/conv_weight/pallas_call | solution.py:625
  168.2 2.7 pad_maximum_fusion.1.grad
  172.1 2.6 constant_dynamic-update-slice_fusion.37
  174.7 2.7 gather_fusion.3
  178.8 30.7 %ffn_forward.1 = (bf16[4096,256]{1,0:T(8,128)(2,1)}, f32[4096,256]{1,0:T(8,128)}, f32[4096,128]{1,0:T(8,128)}, bf16[4096,1024]{1,0:T(8,128)(2,1)}, bf16[4096,102...) custom-call(s32[5]{0:T(128)} %pad_add_fusion.place, bf16[4096,256]{1,0:T(8,128)(2,1)} %get-tuple-element.45.x_ref, ...), custom_call_target="tpu_custom_call" | custom-call | flops 15000000512 | bytes 32000000 | tf_op jit(solution)/shard_map/ffn_forward/pallas_call | solution.py:372
  209.4 2.0 slice.168
  211.4 2.9 slice.167
  216.7 9.8 %conv_weight.2 = f32[3,256,768]{2,1,0:T(8,128)} custom-call(bf16[2,16,128,256]{3,2,1,0:T(8,128)(2,1)} %get-tuple-element.47.joined, bf16[2,20,128,256]{3,2,1,0:T(8,128)(2,1)} %pad_maximum_fusion.1.grad), custom_call_target="tpu_custom_call" | custom-call | flops 4800000000 | bytes 8000000 | tf_op jit(solution)/shard_map/conv_weight/pallas_call | solution.py:625
  226.5 9.7 %conv_data.2 = f32[4,16,8,8,256]{4,3,2,1,0:T(8,128)} custom-call(s32[5]{0:T(128)} %pad_add_fusion.place, bf16[2,20,128,256]{3,2,1,0:T(8,128)(2,1)} %pad_maximum_fusion.1.grad, bf16[3,256,768]{2,1,0:T(8,128)(2,1)} %copy.54.weight), custom_call_target="tpu_custom_call" | custom-call | flops 4800000000 | bytes 8000000 | tf_op jit(solution)/shard_map/conv_data/pallas_call | solution.py:678
  236.2 20.6 %ffn_backward.1 = (f32[4096,256]{1,0:T(8,128)}, bf16[4096,256]{1,0:T(8,128)(2,1)}, f32[256,1024]{1,0:T(8,128)}, f32[256,1024]{1,0:T(8,128)}, f32[256,256]{1,0:T(...) custom-call(f32[4096,256]{1,0:T(8,128)} %bitcast.286, bf16[4096,1024]{1,0:T(8,128)(2,1)} %get-tuple-element.48.act, ...), custom_call_target="tpu_custom_call" | custom-call | flops 19000000512 | bytes 40000000 | tf_op jit(solution)/shard_map/ffn_backward/pallas_call | solution.py:439
  256.8 23.6 %attn_backward.3 = (f32[2,8,128,256]{3,2,1,0:T(8,128)}, f32[256,768]{1,0:T(8,128)}, f32[512,128]{1,0:T(8,128)}, f32[8,256]{1,0:T(8,128)}) custom-call(bf16[4096,256]{1,0:T(8,128)(2,1)} %get-tuple-element.53.mixed, bf16[4096,768]{1,0:T(8,128)(2,1)} %get-tuple-element.54.qkv, bf16[32,512,128]{2,1,0:T(8,128)(2,1)} %get-tuple-element.55.prob, ...), custom_call_target="tpu_custom_call" | custom-call | flops 8000000000 | bytes 16000000 | tf_op jit(solution)/shard_map/attn_backward/pallas_call | solution.py:549
  280.4 23.6 %attn_backward.2 = (f32[2,8,128,256]{3,2,1,0:T(8,128)}, f32[256,768]{1,0:T(8,128)}, f32[512,128]{1,0:T(8,128)}, f32[8,256]{1,0:T(8,128)}) custom-call(bf16[4096,256]{1,0:T(8,128)(2,1)} %get-tuple-element.53.mixed, bf16[4096,768]{1,0:T(8,128)(2,1)} %get-tuple-element.54.qkv, bf16[32,512,128]{2,1,0:T(8,128)(2,1)} %get-tuple-element.55.prob, ...), custom_call_target="tpu_custom_call" | custom-call | flops 8000000000 | bytes 16000000 | tf_op jit(solution)/shard_map/attn_backward/pallas_call | solution.py:549
  306.3 9.5 %conv_data.3 = f32[2,16,128,256]{3,2,1,0:T(8,128)} custom-call(s32[5]{0:T(128)} %pad_add_fusion.place, bf16[2,18,128,256]{3,2,1,0:T(8,128)(2,1)} %pad_maximum_fusion.2.grad, bf16[3,256,768]{2,1,0:T(8,128)(2,1)} %copy.56.weight), custom_call_target="tpu_custom_call" | custom-call | flops 4800000000 | bytes 8000000 | tf_op jit(solution)/shard_map/conv_data/pallas_call | solution.py:678
  318.7 3.1 copy.61
  326.5 3.3 fusion.1
  337.9 2.2 collective-permute-start.31
  343.9 3.7 collective-permute-start.34
  350.4 2.1 slice.253
  371.4 3.5 collective-permute-start.48
  376.8 3.5 collective-permute-start.41
  382.3 2.6 collective-permute-done.40
  391.5 2.0 collective-permute-done.50
  394.5 2.1 collective-permute-start.59
  399.7 3.6 collective-permute-start.55
  405.2 3.6 collective-permute-start.62
  410.8 2.7 collective-permute-done.61
  415.7 2.4 collective-permute-start.66
  418.2 2.5 pad_maximum_fusion
  424.2 4.6 %collective-permute-done.64 = bf16[2,2,144,256]{3,2,1,0:T(8,128)(2,1)S(1)} collective-permute-done((bf16[2,2,144,256]{3,2,1,0:T(8,128)(2,1)S(1)}, bf16[2,2,144,256]{3,2,1,0:T(8,128)(2,1)S(1)}, u32[]{:S(2)}, u32[]{:S(2)}) %collective-permute-start.64) | collective-permute-done | bytes 294944 | tf_op jit(solution)/shard_map/ppermute | solution.py:67
  428.8 3.9 collective-permute-done.66
  434.0 3.3 collective-permute-start.69
  437.3 16.0 %conv_forward.1 = bf16[2,16,128,256]{3,2,1,0:T(8,128)(2,1)} custom-call(s32[5]{0:T(128)} %pad_add_fusion.place, bf16[2,18,128,256]{3,2,1,0:T(8,128)(2,1)} %maximum_select_fusion.1.sums, bf16[2,18,128,256]{3,2,1,0:T(8,128)(2,1)} %copy-done.5, bf16[4608,256]{1,0:T(8,128)(2,1)} %bitcast.229, f32[1,256]{1,0:T(1,128)} %bitcast.285), custom_call_target="tpu_custom_call" | custom-call | flops 9600000000 | bytes 10000000 | tf_op jit(solution)/shard_map/conv_forward/pallas_call | solution.py:718
  (324 shorter events, 151.1 us)
Async XLA Ops:
  2.0 33.8 %collective-permute-start.3 = (bf16[1,8,768]{2,1,0:T(8,128)(2,1)S(1)}, bf16[1,8,768]{2,1,0:T(8,128)(2,1)}, u32[]{:S(2)}, u32[]{:S(2)}) collective-permute-start(bf16[1,8,768]{2,1,0:T(8,128)(2,1)S(1)} %get-tuple-element.108), channel_id=1, source_target_pairs={{0,3},{1,2},{2,1},{3,0},{4,7},{5,6},{6,5},{7,4},{8,11},{9,10},{10,... | collective-permute-start | bytes 36872 | tf_op jit(solution)/shard_map/ppermute | solution.py:67
  7.1 28.8 %collective-permute-start.2 = (bf16[1,8,768]{2,1,0:T(8,128)(2,1)S(1)}, bf16[1,8,768]{2,1,0:T(8,128)(2,1)}, u32[]{:S(2)}, u32[]{:S(2)}) collective-permute-start(bf16[1,8,768]{2,1,0:T(8,128)(2,1)S(1)} %get-tuple-element.108), channel_id=1, source_target_pairs={{0,2},{1,3},{2,0},{3,1},{4,6},{5,7},{6,4},{7,5},{8,10},{9,11},{10,... | collective-permute-start | bytes 36872 | tf_op jit(solution)/shard_map/ppermute | solution.py:67
  7.1 30.3 %collective-permute-start.1 = (bf16[1,8,768]{2,1,0:T(8,128)(2,1)S(1)}, bf16[1,8,768]{2,1,0:T(8,128)(2,1)}, u32[]{:S(2)}, u32[]{:S(2)}) collective-permute-start(bf16[1,8,768]{2,1,0:T(8,128)(2,1)S(1)} %get-tuple-element.108), channel_id=1, source_target_pairs={{0,1},{1,0},{2,3},{3,2},{4,5},{5,4},{6,7},{7,6},{8,9},{9,8},{10,11... | collective-permute-start | bytes 36872 | tf_op jit(solution)/shard_map/ppermute | solution.py:67
  9.7 36.6 %collective-permute-start.9 = (bf16[1,8,1280]{2,1,0:T(8,128)(2,1)}, bf16[1,8,1280]{2,1,0:T(8,128)(2,1)S(1)}, u32[]{:S(2)}, u32[]{:S(2)}) collective-permute-start(bf16[1,8,1280]{2,1,0:T(8,128)(2,1)} %get-tuple-element.188), channel_id=1, source_target_pairs={{0,2},{1,3},{2,0},{3,1},{4,6},{5,7},{6,4},{7,5},{8,10},{9,11},{10,... | collective-permute-start | bytes 61448 | tf_op jit(solution)/shard_map/ppermute | solution.py:67
  12.1 32.8 %collective-permute-start.8 = (bf16[1,8,1280]{2,1,0:T(8,128)(2,1)}, bf16[1,8,1280]{2,1,0:T(8,128)(2,1)}, u32[]{:S(2)}, u32[]{:S(2)}) collective-permute-start(bf16[1,8,1280]{2,1,0:T(8,128)(2,1)} %get-tuple-element.188), channel_id=1, source_target_pairs={{0,1},{1,0},{2,3},{3,2},{4,5},{5,4},{6,7},{7,6},{8,9},{9,8},{10,11... | collective-permute-start | bytes 61448 | tf_op jit(solution)/shard_map/ppermute | solution.py:67
  35.9 10.5 %collective-permute-start.10 = (bf16[1,8,1280]{2,1,0:T(8,128)(2,1)}, bf16[1,8,1280]{2,1,0:T(8,128)(2,1)S(1)}, u32[]{:S(2)}, u32[]{:S(2)}) collective-permute-start(bf16[1,8,1280]{2,1,0:T(8,128)(2,1)} %get-tuple-element.188), channel_id=1, source_target_pairs={{0,3},{1,2},{2,1},{3,0},{4,7},{5,6},{6,5},{7,4},{8,11},{9,10},{10,... | collective-permute-start | bytes 61448 | tf_op jit(solution)/shard_map/ppermute | solution.py:67
  35.9 29.0 %collective-permute-start.16 = (bf16[1,176,256]{2,1,0:T(8,128)(2,1)}, bf16[1,176,256]{2,1,0:T(8,128)(2,1)S(1)}, u32[]{:S(2)}, u32[]{:S(2)}) collective-permute-start(bf16[1,176,256]{2,1,0:T(8,128)(2,1)} %get-tuple-element.157), channel_id=1, source_target_pairs={{0,2},{1,3},{2,0},{3,1},{4,6},{5,7},{6,4},{7,5},{8,10},{9,11},{10,... | collective-permute-start | bytes 270344 | tf_op jit(solution)/shard_map/ppermute | solution.py:67
  37.3 24.2 %collective-permute-start.15 = (bf16[1,176,256]{2,1,0:T(8,128)(2,1)}, bf16[1,176,256]{2,1,0:T(8,128)(2,1)S(1)}, u32[]{:S(2)}, u32[]{:S(2)}) collective-permute-start(bf16[1,176,256]{2,1,0:T(8,128)(2,1)} %get-tuple-element.157), channel_id=1, source_target_pairs={{0,1},{1,0},{2,3},{3,2},{4,5},{5,4},{6,7},{7,6},{8,9},{9,8},{10,11... | collective-permute-start | bytes 270344 | tf_op jit(solution)/shard_map/ppermute | solution.py:67
  44.9 20.0 %collective-permute-start.17 = (bf16[1,176,256]{2,1,0:T(8,128)(2,1)}, bf16[1,176,256]{2,1,0:T(8,128)(2,1)S(1)}, u32[]{:S(2)}, u32[]{:S(2)}) collective-permute-start(bf16[1,176,256]{2,1,0:T(8,128)(2,1)} %get-tuple-element.157), channel_id=1, source_target_pairs={{0,3},{1,2},{2,1},{3,0},{4,7},{5,6},{6,5},{7,4},{8,11},{9,10},{10,... | collective-permute-start | bytes 270344 | tf_op jit(solution)/shard_map/ppermute | solution.py:67
  46.3 101.8 %collective-permute-start.26 = (bf16[2,1,128,256]{3,2,1,0:T(8,128)(2,1)}, bf16[2,1,128,256]{3,2,1,0:T(8,128)(2,1)}, u32[]{:S(2)}, u32[]{:S(2)}) collective-permute-start(bf16[2,1,128,256]{3,2,1,0:T(8,128)(2,1)} %slice.174), channel_id=1, source_target_pairs={{0,28},{4,0},{8,4},{12,8},{16,12},{20,16},{24,20},{28,24},{1,29},{... | collective-permute-start | bytes 393224 | tf_op jit(solution)/shard_map/ppermute | solution.py:124
  46.3 5.6 %collective-permute-start.4 = (bf16[4,8,768]{2,1,0:T(8,128)(2,1)S(1)}, bf16[4,8,768]{2,1,0:T(8,128)(2,1)S(1)}, u32[]{:S(2)}, u32[]{:S(2)}) collective-permute-start(bf16[4,8,768]{2,1,0:T(8,128)(2,1)S(1)} %pad_maximum_fusion.8), channel_id=1, source_target_pairs={{0,8},{1,9},{2,10},{3,11},{4,12},{5,13},{6,14},{7,15},{8,0},{9,1},... | collective-permute-start | bytes 147464 | tf_op jit(solution)/shard_map/ppermute | solution.py:67
  61.0 23.2 %collective-permute-start.23 = (bf16[2,1,128,256]{3,2,1,0:T(8,128)(2,1)}, bf16[2,1,128,256]{3,2,1,0:T(8,128)(2,1)S(1)}, u32[]{:S(2)}, u32[]{:S(2)}) collective-permute-start(bf16[2,1,128,256]{3,2,1,0:T(8,128)(2,1)} %get-tuple-element.117), channel_id=1, source_target_pairs={{0,4},{4,8},{8,12},{12,16},{16,20},{20,24},{24,28},{28,0},{1,5},{5... | collective-permute-start | bytes 393224 | tf_op jit(solution)/shard_map/ppermute | solution.py:124
  61.6 24.4 %collective-permute-start.24 = (bf16[2,1,128,256]{3,2,1,0:T(8,128)(2,1)}, bf16[2,1,128,256]{3,2,1,0:T(8,128)(2,1)S(1)}, u32[]{:S(2)}, u32[]{:S(2)}) collective-permute-start(bf16[2,1,128,256]{3,2,1,0:T(8,128)(2,1)} %get-tuple-element.118), channel_id=1, source_target_pairs={{0,28},{4,0},{8,4},{12,8},{16,12},{20,16},{24,20},{28,24},{1,29},{... | collective-permute-start | bytes 393224 | tf_op jit(solution)/shard_map/ppermute | solution.py:124
  64.9 45.8 %collective-permute-start = (bf16[2,4,128,256]{3,2,1,0:T(8,128)(2,1)}, bf16[2,4,128,256]{3,2,1,0:T(8,128)(2,1)}, u32[]{:S(2)}, u32[]{:S(2)}) collective-permute-start(bf16[2,4,128,256]{3,2,1,0:T(8,128)(2,1)} %slice.162), channel_id=1, source_target_pairs={{0,4},{4,8},{8,12},{12,16},{16,20},{20,24},{24,28},{28,0},{1,5},{5... | collective-permute-start | bytes 1572872 | tf_op jit(solution)/shard_map/ppermute | solution.py:124
  70.1 6.3 %collective-permute-start.12 = (bf16[4,8,1280]{2,1,0:T(8,128)(2,1)S(1)}, bf16[4,8,1280]{2,1,0:T(8,128)(2,1)S(1)}, u32[]{:S(2)}, u32[]{:S(2)}) collective-permute-start(bf16[4,8,1280]{2,1,0:T(8,128)(2,1)S(1)} %pad_maximum_fusion.7), channel_id=1, source_target_pairs={{0,16},{1,17},{2,18},{3,19},{4,20},{5,21},{6,22},{7,23},{8,24},{9,... | collective-permute-start | bytes 245768 | tf_op jit(solution)/shard_map/ppermute | solution.py:67
  81.7 9.7 %collective-permute-start.7 = (bf16[16,8,768]{2,1,0:T(8,128)(2,1)}, bf16[16,8,768]{2,1,0:T(8,128)(2,1)S(1)}, u32[]{:S(2)}, u32[]{:S(2)}) collective-permute-start(bf16[16,8,768]{2,1,0:T(8,128)(2,1)} %get-tuple-element.164), channel_id=1, source_target_pairs={{0,4},{1,5},{2,6},{3,7},{4,0},{5,1},{6,2},{7,3},{8,12},{9,13},{10,... | collective-permute-start | bytes 589832 | tf_op jit(solution)/shard_map/ppermute | solution.py:67
  84.2 23.2 %collective-permute-start.20 = (bf16[4,176,256]{2,1,0:T(8,128)(2,1)}, bf16[4,176,256]{2,1,0:T(8,128)(2,1)}, u32[]{:S(2)}, u32[]{:S(2)}) collective-permute-start(bf16[4,176,256]{2,1,0:T(8,128)(2,1)} %pad_maximum_fusion.4), channel_id=1, source_target_pairs={{0,24},{1,25},{2,26},{3,27},{4,28},{5,29},{6,30},{7,31},{8,16},{9,... | collective-permute-start | bytes 1081352 | tf_op jit(solution)/shard_map/ppermute | solution.py:67
  86.0 19.5 %collective-permute-start.19 = (bf16[4,176,256]{2,1,0:T(8,128)(2,1)}, bf16[4,176,256]{2,1,0:T(8,128)(2,1)}, u32[]{:S(2)}, u32[]{:S(2)}) collective-permute-start(bf16[4,176,256]{2,1,0:T(8,128)(2,1)} %pad_maximum_fusion.4), channel_id=1, source_target_pairs={{0,16},{1,17},{2,18},{3,19},{4,20},{5,21},{6,22},{7,23},{8,24},{9,... | collective-permute-start | bytes 1081352 | tf_op jit(solution)/shard_map/ppermute | solution.py:67
  93.0 11.0 %collective-permute-start.18 = (bf16[4,176,256]{2,1,0:T(8,128)(2,1)}, bf16[4,176,256]{2,1,0:T(8,128)(2,1)S(1)}, u32[]{:S(2)}, u32[]{:S(2)}) collective-permute-start(bf16[4,176,256]{2,1,0:T(8,128)(2,1)} %pad_maximum_fusion.4), channel_id=1, source_target_pairs={{0,8},{1,9},{2,10},{3,11},{4,12},{5,13},{6,14},{7,15},{8,0},{9,1},... | collective-permute-start | bytes 1081352 | tf_op jit(solution)/shard_map/ppermute | solution.py:67
  104.0 44.1 %collective-permute-start.25 = (bf16[2,5,128,256]{3,2,1,0:T(8,128)(2,1)S(1)}, bf16[2,5,128,256]{3,2,1,0:T(8,128)(2,1)S(1)}, u32[]{:S(2)}, u32[]{:S(2)}) collective-permute-start(bf16[2,5,128,256]{3,2,1,0:T(8,128)(2,1)S(1)} %copy-done.19), channel_id=1, source_target_pairs={{0,4},{4,8},{8,12},{12,16},{16,20},{20,24},{24,28},{28,0},{1,5},{5... | collective-permute-start | bytes 1966088 | tf_op jit(solution)/shard_map/ppermute | solution.py:124
  109.3 62.8 %collective-permute-start.21 = (bf16[16,176,256]{2,1,0:T(8,128)(2,1)}, bf16[16,176,256]{2,1,0:T(8,128)(2,1)}, u32[]{:S(2)}, u32[]{:S(2)}) collective-permute-start(bf16[16,176,256]{2,1,0:T(8,128)(2,1)} %get-tuple-element.131), channel_id=1, source_target_pairs={{0,4},{1,5},{2,6},{3,7},{4,0},{5,1},{6,2},{7,3},{8,12},{9,13},{10,... | collective-permute-start | bytes 4325384 | tf_op jit(solution)/shard_map/ppermute | solution.py:67
  325.3 27.9 %collective-permute-start.42 = (bf16[2,2,2,2,8,256]{5,4,3,2,1,0:T(8,128)(2,1)}, bf16[2,2,2,2,8,256]{5,4,3,2,1,0:T(8,128)(2,1)}, u32[]{:S(2)}, u32[]{:S(2)}) collective-permute-start(bf16[2,2,2,2,8,256]{5,4,3,2,1,0:T(8,128)(2,1)} %fusion.24), channel_id=1, source_target_pairs={{0,4},{1,5},{2,6},{3,7},{4,0},{5,1},{6,2},{7,3},{8,12},{9,13},{10,... | collective-permute-start | bytes 196616 | tf_op jit(solution)/shard_map/ppermute | solution.py:67
  336.7 48.9 %collective-permute-start.49 = (bf16[2,2,2,2,8,1024]{5,4,3,2,1,0:T(8,128)(2,1)}, bf16[2,2,2,2,8,1024]{5,4,3,2,1,0:T(8,128)(2,1)}, u32[]{:S(2)}, u32[]{:S(2)}) collective-permute-start(bf16[2,2,2,2,8,1024]{5,4,3,2,1,0:T(8,128)(2,1)} %fusion.10), channel_id=1, source_target_pairs={{0,4},{1,5},{2,6},{3,7},{4,0},{5,1},{6,2},{7,3},{8,12},{9,13},{10,... | collective-permute-start | bytes 786440 | tf_op jit(solution)/shard_map/ppermute | solution.py:67
  336.7 6.2 %collective-permute-start.30 = (f32[40,128]{1,0:T(8,128)S(1)}, f32[40,128]{1,0:T(8,128)S(1)}, u32[]{:S(2)}, u32[]{:S(2)}) collective-permute-start(f32[40,128]{1,0:T(8,128)S(1)} %fusion.67), channel_id=1, source_target_pairs={{0,16},{1,17},{2,18},{3,19},{4,20},{5,21},{6,22},{7,23},{8,24},{9,... | collective-permute-start | bytes 61448 | tf_op jit(solution)/shard_map/ppermute | solution.py:67
  343.9 8.6 %collective-permute-start.34 = (f32[40,128]{1,0:T(8,128)S(1)}, f32[40,128]{1,0:T(8,128)S(1)}, u32[]{:S(2)}, u32[]{:S(2)}) collective-permute-start(f32[40,128]{1,0:T(8,128)S(1)} %add_add_fusion.2), channel_id=1, source_target_pairs={{0,3},{1,2},{2,1},{3,0},{4,7},{5,6},{6,5},{7,4},{8,11},{9,10},{10,... | collective-permute-start | bytes 61448 | tf_op jit(solution)/shard_map/ppermute | solution.py:67
  352.5 36.5 %collective-permute-start.56 = (bf16[2,2,2,2,32,256]{5,4,3,2,1,0:T(8,128)(2,1)}, bf16[2,2,2,2,32,256]{5,4,3,2,1,0:T(8,128)(2,1)}, u32[]{:S(2)}, u32[]{:S(2)}) collective-permute-start(bf16[2,2,2,2,32,256]{5,4,3,2,1,0:T(8,128)(2,1)} %fusion.11), channel_id=1, source_target_pairs={{0,4},{1,5},{2,6},{3,7},{4,0},{5,1},{6,2},{7,3},{8,12},{9,13},{10,... | collective-permute-start | bytes 786440 | tf_op jit(solution)/shard_map/ppermute | solution.py:67
  355.3 7.2 %collective-permute-start.43 = (bf16[2,2,8,256]{3,2,1,0:T(8,128)(2,1)}, bf16[2,2,8,256]{3,2,1,0:T(8,128)(2,1)S(1)}, u32[]{:S(2)}, u32[]{:S(2)}) collective-permute-start(bf16[2,2,8,256]{3,2,1,0:T(8,128)(2,1)} %get-tuple-element.143), channel_id=1, source_target_pairs={{0,8},{1,9},{2,10},{3,11},{4,12},{5,13},{6,14},{7,15},{8,0},{9,1},... | collective-permute-start | bytes 49160 | tf_op jit(solution)/shard_map/ppermute | solution.py:67
  356.3 6.3 %collective-permute-start.45 = (bf16[2,2,8,256]{3,2,1,0:T(8,128)(2,1)}, bf16[2,2,8,256]{3,2,1,0:T(8,128)(2,1)}, u32[]{:S(2)}, u32[]{:S(2)}) collective-permute-start(bf16[2,2,8,256]{3,2,1,0:T(8,128)(2,1)} %get-tuple-element.144), channel_id=1, source_target_pairs={{0,24},{1,25},{2,26},{3,27},{4,28},{5,29},{6,30},{7,31},{8,16},{9,... | collective-permute-start | bytes 49160 | tf_op jit(solution)/shard_map/ppermute | solution.py:67
  367.2 7.8 %collective-permute-start.37 = (bf16[2,2,8,768]{3,2,1,0:T(8,128)(2,1)S(1)}, bf16[2,2,8,768]{3,2,1,0:T(8,128)(2,1)S(1)}, u32[]{:S(2)}, u32[]{:S(2)}) collective-permute-start(bf16[2,2,8,768]{3,2,1,0:T(8,128)(2,1)S(1)} %get-tuple-element.130), channel_id=1, source_target_pairs={{0,16},{1,17},{2,18},{3,19},{4,20},{5,21},{6,22},{7,23},{8,24},{9,... | collective-permute-start | bytes 147464 | tf_op jit(solution)/shard_map/ppermute | solution.py:67
  375.0 6.0 %collective-permute-start.39 = (bf16[8,768]{1,0:T(8,128)(2,1)S(1)}, bf16[8,768]{1,0:T(8,128)(2,1)S(1)}, u32[]{:S(2)}, u32[]{:S(2)}) collective-permute-start(bf16[8,768]{1,0:T(8,128)(2,1)S(1)} %get-tuple-element.146), channel_id=1, source_target_pairs={{0,1},{1,0},{2,3},{3,2},{4,5},{5,4},{6,7},{7,6},{8,9},{9,8},{10,11... | collective-permute-start | bytes 36872 | tf_op jit(solution)/shard_map/ppermute | solution.py:67
  376.8 5.5 %collective-permute-start.41 = (bf16[8,768]{1,0:T(8,128)(2,1)S(1)}, bf16[8,768]{1,0:T(8,128)(2,1)S(1)}, u32[]{:S(2)}, u32[]{:S(2)}) collective-permute-start(bf16[8,768]{1,0:T(8,128)(2,1)S(1)} %get-tuple-element.147), channel_id=1, source_target_pairs={{0,3},{1,2},{2,1},{3,0},{4,7},{5,6},{6,5},{7,4},{8,11},{9,10},{10,... | collective-permute-start | bytes 36872 | tf_op jit(solution)/shard_map/ppermute | solution.py:67
  380.9 33.2 %collective-permute-start.63 = (bf16[2,2,2,2,144,256]{5,4,3,2,1,0:T(8,128)(2,1)}, bf16[2,2,2,2,144,256]{5,4,3,2,1,0:T(8,128)(2,1)S(1)}, u32[]{:S(2)}, u32[]{:S(2)}) collective-permute-start(bf16[2,2,2,2,144,256]{5,4,3,2,1,0:T(8,128)(2,1)} %dynamic-slice_bitcast_fusion), channel_id=1, source_target_pairs={{0,4},{1,5},{2,6},{3,7},{4,0},{5,1},{6,2},{7,3},{8,12},{9,13},{10,... | collective-permute-start | bytes 3538952 | tf_op jit(solution)/shard_map/ppermute | solution.py:67
  382.3 31.8 %collective-permute-start.27 = (bf16[2,4,128,256]{3,2,1,0:T(8,128)(2,1)}, bf16[2,4,128,256]{3,2,1,0:T(8,128)(2,1)S(1)}, u32[]{:S(2)}, u32[]{:S(2)}) collective-permute-start(bf16[2,4,128,256]{3,2,1,0:T(8,128)(2,1)} %slice.253), channel_id=1, source_target_pairs={{0,28},{4,0},{8,4},{12,8},{16,12},{20,16},{24,20},{28,24},{1,29},{... | collective-permute-start | bytes 1572872 | tf_op jit(solution)/shard_map/ppermute | solution.py:124
  386.8 6.6 %collective-permute-start.50 = (bf16[2,2,8,1024]{3,2,1,0:T(8,128)(2,1)S(1)}, bf16[2,2,8,1024]{3,2,1,0:T(8,128)(2,1)S(1)}, u32[]{:S(2)}, u32[]{:S(2)}) collective-permute-start(bf16[2,2,8,1024]{3,2,1,0:T(8,128)(2,1)S(1)} %get-tuple-element.125), channel_id=1, source_target_pairs={{0,8},{1,9},{2,10},{3,11},{4,12},{5,13},{6,14},{7,15},{8,0},{9,1},... | collective-permute-start | bytes 196616 | tf_op jit(solution)/shard_map/ppermute | solution.py:67
  388.0 6.5 %collective-permute-start.52 = (bf16[2,2,8,1024]{3,2,1,0:T(8,128)(2,1)S(1)}, bf16[2,2,8,1024]{3,2,1,0:T(8,128)(2,1)S(1)}, u32[]{:S(2)}, u32[]{:S(2)}) collective-permute-start(bf16[2,2,8,1024]{3,2,1,0:T(8,128)(2,1)S(1)} %get-tuple-element.126), channel_id=1, source_target_pairs={{0,24},{1,25},{2,26},{3,27},{4,28},{5,29},{6,30},{7,31},{8,16},{9,... | collective-permute-start | bytes 196616 | tf_op jit(solution)/shard_map/ppermute | solution.py:67
  389.0 7.7 %collective-permute-start.51 = (bf16[2,2,8,1024]{3,2,1,0:T(8,128)(2,1)S(1)}, bf16[2,2,8,1024]{3,2,1,0:T(8,128)(2,1)S(1)}, u32[]{:S(2)}, u32[]{:S(2)}) collective-permute-start(bf16[2,2,8,1024]{3,2,1,0:T(8,128)(2,1)S(1)} %get-tuple-element.127), channel_id=1, source_target_pairs={{0,16},{1,17},{2,18},{3,19},{4,20},{5,21},{6,22},{7,23},{8,24},{9,... | collective-permute-start | bytes 196616 | tf_op jit(solution)/shard_map/ppermute | solution.py:67
  396.6 6.7 %collective-permute-start.58 = (bf16[2,2,32,256]{3,2,1,0:T(8,128)(2,1)S(1)}, bf16[2,2,32,256]{3,2,1,0:T(8,128)(2,1)S(1)}, u32[]{:S(2)}, u32[]{:S(2)}) collective-permute-start(bf16[2,2,32,256]{3,2,1,0:T(8,128)(2,1)S(1)} %get-tuple-element.124), channel_id=1, source_target_pairs={{0,16},{1,17},{2,18},{3,19},{4,20},{5,21},{6,22},{7,23},{8,24},{9,... | collective-permute-start | bytes 196616 | tf_op jit(solution)/shard_map/ppermute | solution.py:67
  398.3 5.7 %collective-permute-start.53 = (bf16[8,1024]{1,0:T(8,128)(2,1)S(1)}, bf16[8,1024]{1,0:T(8,128)(2,1)S(1)}, u32[]{:S(2)}, u32[]{:S(2)}) collective-permute-start(bf16[8,1024]{1,0:T(8,128)(2,1)S(1)} %get-tuple-element.140), channel_id=1, source_target_pairs={{0,1},{1,0},{2,3},{3,2},{4,5},{5,4},{6,7},{7,6},{8,9},{9,8},{10,11... | collective-permute-start | bytes 49160 | tf_op jit(solution)/shard_map/ppermute | solution.py:67
  399.7 5.5 %collective-permute-start.55 = (bf16[8,1024]{1,0:T(8,128)(2,1)S(1)}, bf16[8,1024]{1,0:T(8,128)(2,1)S(1)}, u32[]{:S(2)}, u32[]{:S(2)}) collective-permute-start(bf16[8,1024]{1,0:T(8,128)(2,1)S(1)} %get-tuple-element.141), channel_id=1, source_target_pairs={{0,3},{1,2},{2,1},{3,0},{4,7},{5,6},{6,5},{7,4},{8,11},{9,10},{10,... | collective-permute-start | bytes 49160 | tf_op jit(solution)/shard_map/ppermute | solution.py:67
  403.3 5.5 %collective-permute-start.54 = (bf16[8,1024]{1,0:T(8,128)(2,1)S(1)}, bf16[8,1024]{1,0:T(8,128)(2,1)S(1)}, u32[]{:S(2)}, u32[]{:S(2)}) collective-permute-start(bf16[8,1024]{1,0:T(8,128)(2,1)S(1)} %get-tuple-element.142), channel_id=1, source_target_pairs={{0,2},{1,3},{2,0},{3,1},{4,6},{5,7},{6,4},{7,5},{8,10},{9,11},{10,... | collective-permute-start | bytes 49160 | tf_op jit(solution)/shard_map/ppermute | solution.py:67
  405.2 5.5 %collective-permute-start.62 = (bf16[32,256]{1,0:T(8,128)(2,1)S(1)}, bf16[32,256]{1,0:T(8,128)(2,1)S(1)}, u32[]{:S(2)}, u32[]{:S(2)}) collective-permute-start(bf16[32,256]{1,0:T(8,128)(2,1)S(1)} %get-tuple-element.138), channel_id=1, source_target_pairs={{0,3},{1,2},{2,1},{3,0},{4,7},{5,6},{6,5},{7,4},{8,11},{9,10},{10,... | collective-permute-start | bytes 49160 | tf_op jit(solution)/shard_map/ppermute | solution.py:67
  409.4 13.0 %collective-permute-start.22 = (bf16[2,5,128,256]{3,2,1,0:T(8,128)(2,1)S(1)}, bf16[2,5,128,256]{3,2,1,0:T(8,128)(2,1)S(1)}, u32[]{:S(2)}, u32[]{:S(2)}) collective-permute-start(bf16[2,5,128,256]{3,2,1,0:T(8,128)(2,1)S(1)} %copy-done.18), channel_id=1, source_target_pairs={{0,28},{4,0},{8,4},{12,8},{16,12},{20,16},{24,20},{28,24},{1,29},{... | collective-permute-start | bytes 1966088 | tf_op jit(solution)/shard_map/ppermute | solution.py:124
  414.6 14.2 %collective-permute-start.64 = (bf16[2,2,144,256]{3,2,1,0:T(8,128)(2,1)S(1)}, bf16[2,2,144,256]{3,2,1,0:T(8,128)(2,1)S(1)}, u32[]{:S(2)}, u32[]{:S(2)}) collective-permute-start(bf16[2,2,144,256]{3,2,1,0:T(8,128)(2,1)S(1)} %get-tuple-element.112), channel_id=1, source_target_pairs={{0,8},{1,9},{2,10},{3,11},{4,12},{5,13},{6,14},{7,15},{8,0},{9,1},... | collective-permute-start | bytes 884744 | tf_op jit(solution)/shard_map/ppermute | solution.py:67
  415.7 17.0 %collective-permute-start.66 = (bf16[2,2,144,256]{3,2,1,0:T(8,128)(2,1)S(1)}, bf16[2,2,144,256]{3,2,1,0:T(8,128)(2,1)S(1)}, u32[]{:S(2)}, u32[]{:S(2)}) collective-permute-start(bf16[2,2,144,256]{3,2,1,0:T(8,128)(2,1)S(1)} %get-tuple-element.113), channel_id=1, source_target_pairs={{0,24},{1,25},{2,26},{3,27},{4,28},{5,29},{6,30},{7,31},{8,16},{9,... | collective-permute-start | bytes 884744 | tf_op jit(solution)/shard_map/ppermute | solution.py:67
  418.1 14.6 %collective-permute-start.65 = (bf16[2,2,144,256]{3,2,1,0:T(8,128)(2,1)S(1)}, bf16[2,2,144,256]{3,2,1,0:T(8,128)(2,1)S(1)}, u32[]{:S(2)}, u32[]{:S(2)}) collective-permute-start(bf16[2,2,144,256]{3,2,1,0:T(8,128)(2,1)S(1)} %get-tuple-element.114), channel_id=1, source_target_pairs={{0,16},{1,17},{2,18},{3,19},{4,20},{5,21},{6,22},{7,23},{8,24},{9,... | collective-permute-start | bytes 884744 | tf_op jit(solution)/shard_map/ppermute | solution.py:67
  432.9 20.4 %collective-permute-start.67 = (bf16[144,256]{1,0:T(8,128)(2,1)S(1)}, bf16[144,256]{1,0:T(8,128)(2,1)S(1)}, u32[]{:S(2)}, u32[]{:S(2)}) collective-permute-start(bf16[144,256]{1,0:T(8,128)(2,1)S(1)} %get-tuple-element.119), channel_id=1, source_target_pairs={{0,1},{1,0},{2,3},{3,2},{4,5},{5,4},{6,7},{7,6},{8,9},{9,8},{10,11... | collective-permute-start | bytes 221192 | tf_op jit(solution)/shard_map/ppermute | solution.py:67
  434.0 19.3 %collective-permute-start.69 = (bf16[144,256]{1,0:T(8,128)(2,1)S(1)}, bf16[144,256]{1,0:T(8,128)(2,1)S(1)}, u32[]{:S(2)}, u32[]{:S(2)}) collective-permute-start(bf16[144,256]{1,0:T(8,128)(2,1)S(1)} %get-tuple-element.120), channel_id=1, source_target_pairs={{0,3},{1,2},{2,1},{3,0},{4,7},{5,6},{6,5},{7,4},{8,11},{9,10},{10,... | collective-permute-start | bytes 221192 | tf_op jit(solution)/shard_map/ppermute | solution.py:67
  437.3 16.0 %collective-permute-start.68 = (bf16[144,256]{1,0:T(8,128)(2,1)S(1)}, bf16[144,256]{1,0:T(8,128)(2,1)S(1)}, u32[]{:S(2)}, u32[]{:S(2)}) collective-permute-start(bf16[144,256]{1,0:T(8,128)(2,1)S(1)} %get-tuple-element.121), channel_id=1, source_target_pairs={{0,2},{1,3},{2,0},{3,1},{4,6},{5,7},{6,4},{7,5},{8,10},{9,11},{10,... | collective-permute-start | bytes 221192 | tf_op jit(solution)/shard_map/ppermute | solution.py:67
  (60 other events, 503.9 us)
